TPU v7x, 32 devices: a whole 2x2x4 slice. The times are simulated.
32 devices in a mesh: dp: 8 (over y, x, core), fsdp: 4 (over z).
Axes of the slice: x: 2, y: 2, z: 4, core: 2. Of those that a mesh axis runs over, the one named last changes fastest.
Arguments:
- tokens: bfloat16 [30336, 768], P(('dp', 'fsdp')), may hold values from -6 to 6
- modality: int32 [30336], P(('dp', 'fsdp')), may hold values from 0 to 1, as said below
- token_mask: int32 [30336], P(('dp', 'fsdp')), may hold values from 0 to 1, as said below
- cotangent: bfloat16 [30336, 768], P(('dp', 'fsdp')), may hold values from -6 to 6
- mask_vector: bfloat16 [768], replicated, may hold values from -4 to 4
- ln_one_gain: bfloat16 [768], P(('dp', 'fsdp')), may hold values from 0.25 to 1.75
- ln_one_shift: bfloat16 [768], P(('dp', 'fsdp')), may hold values from -3 to 3
- w_qkv: bfloat16 [768, 2304], P(('dp', 'fsdp')), may hold values from -0.21875 to 0.21875
- w_out: bfloat16 [768, 768], P(('dp', 'fsdp')), may hold values from -1.75 to 1.75
- ln_two_gain: bfloat16 [768], P(('dp', 'fsdp')), may hold values from 0.25 to 1.75
- ln_two_shift: bfloat16 [768], P(('dp', 'fsdp')), may hold values from -3 to 3
- w_up: bfloat16 [2, 768, 3072], P(None, ('dp', 'fsdp')), may hold values from -0.21875 to 0.21875
- w_down: bfloat16 [2, 3072, 768], P(None, ('dp', 'fsdp')), may hold values from -0.109375 to 0.109375
Outputs:
- output: bfloat16 [30336, 768], P(('dp', 'fsdp'))
- grad_tokens: float32 [30336, 768], P(('dp', 'fsdp'))
- grad_mask_vector: float32 [768], replicated
- grad_ln_one_gain: float32 [768], P(('dp', 'fsdp'))
- grad_ln_one_shift: float32 [768], P(('dp', 'fsdp'))
- grad_w_qkv: float32 [768, 2304], P(('dp', 'fsdp'))
- grad_w_out: float32 [768, 768], P(('dp', 'fsdp'))
- grad_ln_two_gain: float32 [768], P(('dp', 'fsdp'))
- grad_ln_two_shift: float32 [768], P(('dp', 'fsdp'))
- grad_w_up: float32 [768, 3072], P(('dp', 'fsdp'))
- grad_w_down: float32 [3072, 768], P(('dp', 'fsdp'))
Inputs may be any that keep to these rules, and one draw needn't show every extreme that they name: `modality`: in each of the 128 sequences of 237 consecutive tokens, either the first 197 tokens are image tokens (0) and the last 40 are text tokens (1), or all 237 are text tokens. `token_mask`: 1 only at text tokens (where modality is 1).
All inputs are finite; a program needn't handle non-finite values.
Results may differ from a plain program's by a relative error of at most 0.011.
Values may be sent and summed in bfloat16 or wider, within the bound.
No kernel may reach another device: no remote copies, remote signals or barrier semaphores. Data moves between devices by JAX's collectives and lax.ppermute only.
A program may use at most 192 MiB of HBM per device.

v0:
```python
import functools
import math

import jax
import jax.numpy as jnp
from jax import lax
from jax.experimental import pallas as pl
from jax.experimental.pallas import tpu as pltpu
from jax.sharding import Mesh, PartitionSpec as P

H = 12
HD = 64
LEN = 237
PATCHES = 197
HEAD = 208
TAIL = 48
SEQ = HEAD + TAIL
D = H * HD
FF = 4 * D
BLK = 256
EPS = 1e-05
F32 = jnp.float32
BF16 = jnp.bfloat16
MIB = 1 << 20
ROWS_ONE = 864
ROWS_QKV = 304


def dot(a, b):
    return jnp.dot(a, b, preferred_element_type=F32)


def dot_nt(a, b):
    return lax.dot_general(a, b, (((1,), (1,)), ((), ())), preferred_element_type=F32)


def dot_tn(a, b):
    return lax.dot_general(a, b, (((0,), (0,)), ((), ())), preferred_element_type=F32)


def mean(rows):
    return jnp.mean(rows, -1, keepdims=True)


def normalize(rows):
    centred = rows - mean(rows)
    inverse = lax.rsqrt(mean(centred * centred) + EPS)
    return centred * inverse, inverse


def normalize_back(grad, unit, inverse, gain):
    scaled = grad * gain
    return inverse * (scaled - mean(scaled) - unit * mean(scaled * unit))


def total(rows):
    return jnp.sum(rows, 0, keepdims=True)


def halves(pair):
    lane = lax.broadcasted_iota(jnp.int32, pair.shape, 1)
    zero = jnp.zeros_like(pair)
    return jnp.concatenate(
        [jnp.where(lane < HD, pair, zero), jnp.where(lane < HD, zero, pair)], 0
    )


def key_bias():
    key = lax.broadcasted_iota(jnp.int32, (1, SEQ), 1)
    valid = (key < PATCHES) | ((key >= HEAD) & (key < HEAD + LEN - PATCHES))
    return jnp.where(valid, 0.0, -1e30)


def softmax_pair(queries, keys_cat, bias):
    scores = dot_nt(queries, keys_cat)
    out = []
    for head in range(2):
        own = scores[:, head * SEQ : (head + 1) * SEQ] + bias
        powers = jnp.exp(own - jnp.max(own, -1, keepdims=True))
        out.append(powers * (1.0 / jnp.sum(powers, -1, keepdims=True)))
    return jnp.concatenate(out, 1)


def spans(where_ref, pieces, rows):
    if len(pieces) == 8:
        for j in range(8):
            yield pieces[j], where_ref[j], 0, rows
        return
    for side in range(2):
        for j in range(5):
            block = where_ref[4 * side + min(j, 3)]
            size = rows if j < 3 else rows // 2
            yield pieces[5 * side + j], block, (size if j == 4 else 0), size


def started(copies, sems, start=True):
    copies = [
        pltpu.make_async_copy(source, target, sems.at[j])
        for j, (source, target) in enumerate(copies)
    ]
    if start:
        for copy in copies:
            copy.start()
    return copies


def load_pieces(where_ref, pieces, target, sems, columns, start=True):
    return started(
        [
            (
                piece.at[:, pl.ds(columns[0], columns[1])],
                target.at[pl.ds(pl.multiple_of(block * 96 + first, 16), size), :],
            )
            for piece, block, first, size in spans(where_ref, pieces, 96)
        ],
        sems,
        start,
    )


def load_expert(where_ref, pieces, up, down, sems):
    copies = []
    for piece, block, first, size in spans(where_ref, pieces, 768):
        if first == 0:
            for chunk in range(4):
                copies.append(
                    (
                        piece.at[pl.ds(chunk * 96, 96), :],
                        up.at[chunk, pl.ds(pl.multiple_of(block * 96, 96), 96), :],
                    )
                )
        if first + size == 768:
            copies.append(
                (
                    piece.at[pl.ds(384 - first, 384), :],
                    down.at[pl.ds(pl.multiple_of(block * 384, 384), 384), :],
                )
            )
    return started(copies, sems)


def wait_all(copies):
    for copy in copies:
        copy.wait()


def attention_kernel(where_ref, tokens, masked, vector, *rest):
    pieces, rest = rest[:8], rest[8:]
    qkv, softs, context, normed_one, params, weights, sems = rest

    @pl.when(pl.program_id(0) == 0)
    def _():
        wait_all(load_pieces(where_ref, pieces, weights, sems, (0, weights.shape[1])))
        columns = weights[:, 4 * D : 4 * D + 128].astype(F32)
        params[...] = jnp.transpose(columns)[:8]

    start = jnp.where(masked[...] == 1.0, vector[...], tokens[...].astype(F32))
    unit, _ = normalize(start)
    first = (unit * params[0:1] + params[1:2]).astype(BF16)
    normed_one[...] = first
    for third in range(3):
        at = pl.ds(third * D, D)
        qkv[:, at] = dot(first, weights[:, at]).astype(BF16)
    bias = key_bias()
    for pair in range(H // 2):
        queries = qkv[:, pl.ds(pair * 128, 128)] * BF16(1.0 / math.sqrt(HD))
        keys = halves(qkv[:, pl.ds(D + pair * 128, 128)])
        values = halves(qkv[:, pl.ds(2 * D + pair * 128, 128)])
        soft = softmax_pair(queries, keys, bias)
        softs[0, pair] = soft
        attention = soft.astype(BF16)
        context[:, pl.ds(pair * 128, 128)] = dot(attention, values).astype(BF16)


def chosen(place, block):
    row = lax.broadcasted_iota(jnp.int32, (BLK, place.shape[1]), 0) + block * BLK
    return jnp.where(row == place[...], 1.0, 0.0).astype(BF16)


def rows_of(block):
    return pl.ds(pl.multiple_of(block * BLK, BLK), BLK)


def feed_back_kernel(where_ref, place, vector, cotangent, context, params, *rest):
    pieces, attention_pieces, rest = rest[:10], rest[10:18], rest[18:]
    keep, send, send_far, grad_context, sums = rest[:5]
    rows_two, rows_hidden, rows_cot, rows_context, grad_two = rest[5:10]
    (sum_up, sum_down, w_up, w_down, w_out, stage) = rest[10:16]
    sems, attention_sems, out_sems = rest[16:]
    step = pl.program_id(0)
    blocks = where_ref[10]
    core = where_ref[8]

    @pl.when(step == 0)
    def _():
        copies = load_pieces(where_ref, attention_pieces, w_out, attention_sems, (3 * D, D))
        more = load_expert(where_ref, pieces, w_up, w_down, sems)

        def gather(block, _):
            pick, at = chosen(place, block), rows_of(block)
            rows_cot[at, :] = dot(pick, cotangent[...]).astype(BF16)
            rows_context[at, :] = dot(pick, context[...]).astype(BF16)
            grad_two[at, :] = jnp.zeros((BLK, D), F32)
            return 0

        def norm(block, _):
            at = rows_of(block)
            rows = vector[...] + dot(rows_context[at, :], w_out[...])
            rows_hidden[at, :] = rows
            unit, _ = normalize(rows)
            rows_two[at, :] = (unit * params[2:3] + params[3:4]).astype(BF16)
            return 0

        lax.fori_loop(0, blocks, gather, 0)
        wait_all(copies)
        lax.fori_loop(0, blocks, norm, 0)
        wait_all(more)

    up = w_up.at[step]
    down = w_down.at[pl.ds(pl.multiple_of(step * D, D), D), :]

    def expert(block, _):
        at = rows_of(block)
        rows, grads = rows_two[at, :], rows_cot[at, :]
        pre = dot(rows, up[...])
        chance = 0.5 * (1.0 + lax.erf(pre * math.sqrt(0.5)))
        activated = (pre * chance).astype(BF16)
        slope = chance + pre * (jnp.exp(-0.5 * pre * pre) * (1.0 / math.sqrt(2.0 * math.pi)))
        grad_pre = (dot_nt(grads, down[...]) * slope).astype(BF16)
        grad_two[at, :] += dot_nt(grad_pre, up[...])
        add_down = dot_tn(activated, grads)
        add_up = dot_tn(rows, grad_pre)

        @pl.when(block == 0)
        def _():
            sum_down[...] = add_down
            sum_up[...] = add_up

        @pl.when(block > 0)
        def _():
            sum_down[...] += add_down
            sum_up[...] += add_up

        return 0

    lax.fori_loop(0, blocks, expert, 0)

    def leaving(at_step):
        rows = pl.ds(pl.multiple_of(at_step * 96, 96), 96)
        columns = pl.ds(384, 384)
        mine = jnp.bitwise_xor(at_step, where_ref[9])
        near = jnp.minimum(mine, 2)
        sem = out_sems.at[at_step]
        return [
            (None, stage.at[0, :, rows, :], keep.at[:, rows, :], sem.at[0]),
            (None, stage.at[0, mine, columns, :], keep.at[mine, columns, :], sem.at[1]),
            (None, stage.at[1, pl.ds(0, 3), rows, :], send.at[:, rows, :], sem.at[2]),
            (None, stage.at[1, 3, rows, :], send_far.at[rows, :], sem.at[3]),
            (mine < 3, stage.at[1, near, columns, :], send.at[near, columns, :], sem.at[4]),
            (mine == 3, stage.at[1, 3, columns, :], send_far.at[columns, :], sem.at[4]),
        ]

    def each(copies, act):
        for when, source, target, sem in copies:
            copy = pltpu.make_async_copy(source, target, sem)
            if when is None:
                act(copy)
            else:
                pl.when(when)(functools.partial(act, copy))

    up_at = pl.ds(pl.multiple_of(step * 96, 96), 96)
    mine = jnp.bitwise_xor(step, where_ref[9])
    for side in range(2):
        for j in range(4):
            source = pl.ds(pl.multiple_of(where_ref[4 * side + j] * 96, 96), 96)
            stage[side, j, up_at, :] = sum_up[source, :].astype(BF16)
        half = core if side == 0 else 1 - core
        source = pl.ds(pl.multiple_of(half * 384, 384), 384)
        stage[side, mine, pl.ds(384, 384), :] = sum_down[source, :].astype(BF16)
    each(leaving(step), lambda copy: copy.start())

    @pl.when(step == pl.num_programs(0) - 1)
    def _():
        sums[...] = jnp.zeros_like(sums)

        def back(block, _):
            pick, at = chosen(place, block), rows_of(block)
            unit, inverse = normalize(rows_hidden[at, :])
            grad = grad_two[at, :]
            grad_hidden = rows_cot[at, :].astype(F32) + normalize_back(
                grad, unit, inverse, params[2:3]
            )
            sums[0:1] += total(grad * unit)
            sums[1:2] += total(grad)
            sums[2:3] += total(grad_hidden)
            grad_attn = grad_hidden.astype(BF16)
            add_out = dot_tn(rows_context[at, :], grad_attn)
            rows = dot_nt(grad_attn, w_out[...]).astype(BF16)
            rows = dot_tn(pick, rows).astype(BF16)

            @pl.when(block == 0)
            def _():
                sum_up[...] = add_out
                grad_context[...] = rows

            @pl.when(block > 0)
            def _():
                sum_up[...] += add_out
                grad_context[...] += rows

            return 0

        lax.fori_loop(0, blocks, back, 0)
        for side in range(2):
            for j in range(4):
                source = pl.ds(pl.multiple_of(where_ref[4 * side + j] * 96, 96), 96)
                stage[side, j, pl.ds(768, 96), :] = sum_up[source, :].astype(BF16)
        rows = pl.ds(768, 96)
        sem = out_sems.at[4]
        last = [
            (None, stage.at[0, :, rows, :], keep.at[:, rows, :], sem.at[0]),
            (None, stage.at[1, pl.ds(0, 3), rows, :], send.at[:, rows, :], sem.at[1]),
            (None, stage.at[1, 3, rows, :], send_far.at[rows, :], sem.at[2]),
        ]
        each(last, lambda copy: copy.start())
        each(last, lambda copy: copy.wait())
        for at_step in range(4):
            each(leaving(at_step), lambda copy: copy.wait())


def put_rows(target, rows, seq):
    target[seq * LEN : seq * LEN + PATCHES] = rows[:PATCHES]
    target[seq * LEN + PATCHES : (seq + 1) * LEN] = rows[HEAD : HEAD + LEN - PATCHES]


def attention_back_kernel(
    where_ref, qkv, softs, grad_context, normed_one, tokens, masked, vector, params, before, *rest
):
    pieces = rest[:8]
    keep, send, grad_tokens = rest[8:11]
    weights, sums, grad_qkv, stage, sems, out_sems = rest[11:]
    step = pl.program_id(0)
    here = pl.ds(pl.multiple_of(step * SEQ, SEQ), SEQ)

    def copies():
        return load_pieces(where_ref, pieces, weights, sems, (0, 3 * D), False)

    @pl.when(step == 0)
    def _():
        for copy in copies():
            copy.start()
        sums[...] = before[...]

    inv_root = 1.0 / math.sqrt(HD)
    top = lax.broadcasted_iota(jnp.int32, (128, SEQ), 0) < HD
    for pair in range(H // 2):
        queries = qkv[:, pl.ds(pair * 128, 128)]
        keys = halves(qkv[:, pl.ds(D + pair * 128, 128)])
        values = halves(qkv[:, pl.ds(2 * D + pair * 128, 128)])
        grads = grad_context[:, pl.ds(pair * 128, 128)]
        grad_soft = dot_nt(grads, values)
        parts = []
        for head in range(2):
            span = slice(head * SEQ, (head + 1) * SEQ)
            own, grad = softs[0, pair, :, span], grad_soft[:, span]
            parts.append(own * (grad - jnp.sum(own * grad, -1, keepdims=True)))
        grad_scores = jnp.concatenate(parts, 1).astype(BF16)
        grad_qkv[here, pl.ds(pair * 128, 128)] = (dot(grad_scores, keys) * inv_root).astype(BF16)
        by_key = dot_tn(queries, grad_scores) * inv_root
        by_key = jnp.where(top, by_key[:, :SEQ], by_key[:, SEQ:])
        grad_qkv[here, pl.ds(D + pair * 128, 128)] = jnp.transpose(by_key).astype(BF16)
        by_value = dot_tn(grads, softs[0, pair].astype(BF16))
        by_value = jnp.where(top, by_value[:, :SEQ], by_value[:, SEQ:])
        grad_qkv[here, pl.ds(2 * D + pair * 128, 128)] = jnp.transpose(by_value).astype(BF16)

    @pl.when(step == 0)
    def _():
        wait_all(copies())

    grad_one = dot_nt(grad_qkv[here, :], weights[...])
    start = jnp.where(masked[...] == 1.0, vector[...], tokens[...].astype(F32))
    unit, inverse = normalize(start)
    grad_start = normalize_back(grad_one, unit, inverse, params[0:1])
    sums[3:4] += total(grad_one * unit)
    sums[4:5] += total(grad_one)
    sums[2:3] += total(jnp.where(masked[...] == 1.0, grad_start, 0.0))
    kept = jnp.where(masked[...] == 1.0, 0.0, grad_start)
    for seq in range(normed_one.shape[0] // SEQ):
        pl.when(step == seq)(functools.partial(put_rows, grad_tokens, kept, seq))

    @pl.when(step == pl.num_programs(0) - 1)
    def _():
        extra = jnp.concatenate([sums[...], jnp.zeros_like(sums[...])], 0).astype(BF16)
        for third in range(3):
            for part in range(3):
                at = pl.ds(third * D + part * SEQ, SEQ)
                add = dot_tn(normed_one[...], grad_qkv[:, at]).astype(BF16)
                for block in range(8):
                    stage[block, pl.ds(third * 96, 96), pl.ds(part * SEQ, SEQ)] = add[
                        block * 96 : (block + 1) * 96
                    ]
        out_copies = []
        for side, out in enumerate((keep, send)):
            for j in range(4):
                block = where_ref[4 * side + j]
                stage[block, pl.ds(3 * 96, 16), :] = extra
                out_copies.append((stage.at[block], out.at[j]))
        wait_all(started(out_copies, out_sems))


def gelu(pre):
    return (pre * (0.5 * (1.0 + lax.erf(pre * math.sqrt(0.5))))).astype(BF16)


def feed(text, where_ref, rows_in, sums, up, down, tails):
    seqs = rows_in.shape[0] // SEQ
    for seq in range(seqs):
        head = pl.ds(seq * SEQ, HEAD)

        @pl.when(where_ref[11 + seq] == int(text))
        def _():
            activated = gelu(dot(rows_in[head, :], up[...]))
            sums[head, :] += dot(activated, down[...])

    if text:
        more = dot(gelu(dot(tails[...], up[...])), down[...])
        for seq in range(seqs):
            sums[pl.ds(seq * SEQ + HEAD, TAIL), :] += more[seq * TAIL : (seq + 1) * TAIL]


def feed_text_kernel(where_ref, tokens, masked, vector, context, params, *rest):
    pieces, attention_pieces, rest = rest[:10], rest[10:18], rest[18:]
    out, normed_two, w_up, w_down, w_out, sems, attention_sems, tails = rest
    step = pl.program_id(0)

    @pl.when(step == 0)
    def _():
        copies = load_pieces(where_ref, attention_pieces, w_out, attention_sems, (3 * D, D))
        more = load_expert(where_ref, pieces, w_up, w_down, sems)
        wait_all(copies)
        for seq in range(tokens.shape[0] // SEQ):
            at = pl.ds(seq * SEQ, SEQ)
            start = jnp.where(masked[at, :] == 1.0, vector[...], tokens[at, :].astype(F32))
            hidden = start + dot(context[at, :], w_out[...])
            out[at, :] = hidden
            unit, _ = normalize(hidden)
            second = (unit * params[2:3] + params[3:4]).astype(BF16)
            normed_two[at, :] = second
            tails[pl.ds(seq * TAIL, TAIL), :] = second[HEAD:]
        wait_all(more)

    down = w_down.at[pl.ds(pl.multiple_of(step * D, D), D), :]
    feed(True, where_ref, normed_two, out, w_up.at[step], down, tails)


def feed_image_kernel(where_ref, rows_in, before, *rest):
    pieces, (out, sums, w_up, w_down, sems, flat) = rest[:10], rest[10:]
    step = pl.program_id(0)

    @pl.when(step == 0)
    def _():
        copies = load_expert(where_ref, pieces, w_up, w_down, sems)
        sums[...] = before[...]
        wait_all(copies)

    down = w_down.at[pl.ds(pl.multiple_of(step * D, D), D), :]
    feed(False, where_ref, rows_in, sums, w_up.at[step], down, None)

    @pl.when(step == pl.num_programs(0) - 1)
    def _():
        for seq in range(rows_in.shape[0] // SEQ):
            put_rows(flat, sums[pl.ds(seq * SEQ, SEQ), :], seq)
        out[...] = flat[...].astype(BF16)


def whole(shape):
    return pl.BlockSpec(shape, lambda *_: (0,) * len(shape), pipeline_mode=pl.Buffered(1))


def by_step(shape):
    return pl.BlockSpec(shape, lambda i, *_: (i,) + (0,) * (len(shape) - 1))


ANY = pl.BlockSpec(memory_space=pl.ANY)


def call(kernel, steps, ins, in_specs, outs, out_specs, scratch, name):
    run = pl.pallas_call(
        kernel,
        out_shape=tuple(jax.ShapeDtypeStruct(s, d) for s, d in outs),
        grid_spec=pltpu.PrefetchScalarGridSpec(
            num_scalar_prefetch=1,
            grid=(steps,),
            in_specs=in_specs,
            out_specs=out_specs,
            scratch_shapes=scratch,
        ),
        compiler_params=pltpu.CompilerParams(vmem_limit_bytes=60 * MIB),
        cost_estimate=pl.CostEstimate(flops=1, bytes_accessed=1, transcendentals=0),
        name=name,
    )
    return run(*ins)


def lay(rows, seqs):
    rows = rows.reshape(seqs, LEN, -1)
    return jnp.concatenate(
        [
            jnp.pad(rows[:, :PATCHES], ((0, 0), (0, HEAD - PATCHES), (0, 0))),
            jnp.pad(rows[:, PATCHES:], ((0, 0), (0, TAIL - LEN + PATCHES), (0, 0))),
        ],
        1,
    ).reshape(seqs * SEQ, -1)


def tie(*trees):
    return lax.optimization_barrier(trees)


def in_order(rows, part, blocks=0, axis=0):
    rows = jnp.moveaxis(rows, axis, blocks)
    shape, columns = rows.shape[:blocks], rows.shape[-1]
    count, size = rows.shape[blocks], rows.shape[blocks + 1]
    if size == part:
        return rows.reshape(*shape, count * part, columns)
    up = rows[..., : 4 * part, :].reshape(*shape, count, 4, part, columns)
    up = jnp.swapaxes(up, blocks, blocks + 1).reshape(*shape, 4 * count * part, columns)
    down = rows[..., 4 * part :, :].reshape(*shape, count * (size - 4 * part), columns)
    return jnp.concatenate([up, down], -2)


class Cube:
    axes = ("y", "x", "core", "z")
    swap = [(0, 1), (1, 0)]

    def __init__(self):
        y, x, core, z = (lax.axis_index(a) for a in self.axes)
        self.z, self.core, self.flat = z, core, y * 2 + x
        self.index = ((y * 2 + x) * 2 + core) * 4 + z

    def turn(self, block, k):
        return lax.ppermute(block, "z", [(i, (i + k) % 4) for i in range(4)])

    def turns(self, block):
        return [block] + [self.turn(block, k) for k in (1, 2, 3)]

    def ring(self, ring, part):
        out = []
        for place in range(4):
            k = lax.rem(self.z + 4 - place, 4)
            out.append(
                jnp.where(
                    k == 0,
                    ring[0],
                    jnp.where(k == 1, ring[1], jnp.where(k == 2, ring[2], ring[3])),
                )
            )
        return in_order(jnp.stack(out), part)

    def swapped(self, block, axis):
        return lax.ppermute(block, axis, self.swap)

    def sides(self, own):
        return own, self.swapped(own, "x"), self.swapped(own, "y")

    def halves(self, near):
        half = near[0].shape[0] // 2
        return near[1][:half], near[2][half:]

    def to_corners(self, near, halves):
        return (*near, self.swapped(halves[0], "y"), self.swapped(halves[1], "x"))

    def corner(self, near):
        return self.to_corners(near, self.halves(near))

    def cores(self, near):
        return [*near] + [self.swapped(b, "core") for b in near]

    def plane(self, j, block):
        if j == 1:
            return self.swapped(block, "x")
        if j == 2:
            return self.swapped(block, "y")
        return lax.ppermute(block, ("y", "x"), [(i, 3 - i) for i in range(4)])

    def to_core(self, block):
        return self.swapped(block, "core")

    def far_sums(self, keep, got):
        half = got.shape[0] // 2
        return [
            (keep[3, at].astype(F32) + got[at].astype(F32)).astype(BF16)
            for at in (slice(half), slice(half, None))
        ]

    def to_corner(self, both):
        return self.swapped(both[0], "x"), self.swapped(both[1], "y")

    def side_sums(self, keep, got, corner):
        half = corner[0].shape[0]
        by_x = jnp.pad(corner[0], ((0, half), (0, 0))).astype(F32)
        by_y = jnp.pad(corner[1], ((half, 0), (0, 0))).astype(F32)
        to_x = keep[1].astype(F32) + got[1].astype(F32) + by_y
        to_y = keep[2].astype(F32) + got[2].astype(F32) + by_x
        return [keep, got, to_x.astype(BF16), to_y.astype(BF16)]

    def to_sides(self, sums):
        return [*sums[:2], self.swapped(sums[2], "x"), self.swapped(sums[3], "y")]

    def plane_sums(self, keep, got, rows):
        both = [keep[j, :rows].astype(F32) + got[j, :rows].astype(F32) for j in (1, 2, 3)]
        return [keep, got] + [b.astype(BF16) for b in both]

    def to_plane(self, sums):
        return sums[:2] + [self.plane(j, sums[j + 1]) for j in (1, 2, 3)]

    def square(self, own):
        return [own] + [self.plane(j, own) for j in (1, 2, 3)]

    def square_cores(self, near):
        return [*near] + [self.swapped(b, "core") for b in near]

    def last(self, near):
        return near[3:]

    def cores_of(self, near, last):
        return self.cores([*near[:3], *last])

    def far_cores(self, near):
        return [self.swapped(b, "core") for b in near]

    def all_cores(self, near, far, last):
        return [*near, *far, *last]

    def ring_sums(self, group, fields):
        keep, got, *more = group
        rows = more[0].shape[0]
        mine = sum(m.astype(F32) for m in (keep[0, :rows], got[0, :rows], *more))
        rounded = lax.optimization_barrier(mine.astype(BF16))
        return [cut(mine, fields, self.z)] + [
            cut(rounded, fields, lax.rem(self.z + k, 4)) for k in (1, 2, 3)
        ]

    def to_ring(self, parts, which):
        return [self.turn(p, k) if k in which else p for k, p in enumerate(parts)]

    def add_ring(self, ring):
        return ring[0] + sum(m.astype(F32) for m in ring[1:])


class Flat:
    axes = ("dp", "fsdp")

    def __init__(self, count):
        self.flat = self.core = jnp.int32(0)
        self.index = lax.axis_index(self.axes)
        self.count = count

    def turns(self, block):
        return lax.all_gather(block, self.axes, axis=0)

    def ring(self, full, part):
        return in_order(full.reshape((8, -1) + full.shape[1:]), part, 1, 1)

    def sides(self, own):
        return own

    def halves(self, near):
        return ()

    def to_corners(self, near, halves):
        return near

    def corner(self, near):
        return near

    def cores(self, near):
        half = near.shape[1] // 2
        out = []
        for side in range(2):
            out += [near[side], near[2 + side], near[4 + side]]
            out += [near[6 + side, :half], near[6 + side, half:]]
        return out

    def to_core(self, block):
        return block

    def far_sums(self, keep, got):
        return got

    def to_corner(self, both):
        return both

    def side_sums(self, keep, got, corner):
        return self.plane_sums(keep, jnp.concatenate([got, corner[None]]), None)

    def to_sides(self, sums):
        return sums

    def plane_sums(self, keep, got, rows):
        return [jnp.stack([keep, got], 1).reshape((8,) + keep.shape[1:])]

    def to_plane(self, sums):
        return sums

    def square(self, own):
        return own

    def square_cores(self, near):
        return [near[b] for b in (0, 2, 4, 6, 1, 3, 5, 7)]

    def last(self, near):
        return ()

    def cores_of(self, near, last):
        return self.cores(near)

    def far_cores(self, near):
        return ()

    def all_cores(self, near, far, last):
        return self.cores(near)

    def ring_sums(self, group, fields):
        ways = self.count // 8
        parts = [[cut(block, fields, w, ways) for w in range(ways)] for block in group[0]]
        return jnp.stack([p for block in parts for p in block]).astype(F32)

    def to_ring(self, parts, which):
        if 3 not in which:
            return parts
        return lax.psum_scatter(parts, self.axes, scatter_dimension=0, tiled=False)

    def add_ring(self, ring):
        return ring


def pack_expert(up, down):
    part = up.shape[0]
    up = up.reshape(part, 4, D).transpose(1, 0, 2).reshape(4 * part, D)
    return jnp.concatenate([up, down], 0)


def cut(rows, fields, place, ways=4):
    out, at = [], 0
    for groups, size in fields:
        part = rows[at : at + max(groups, 1) * size]
        at += max(groups, 1) * size
        if groups:
            part = part.reshape(groups, ways, size // ways, D)
            part = lax.dynamic_index_in_dim(part, place, 1, keepdims=False).reshape(-1, D)
        out.append(part)
    return jnp.concatenate(out)


def layer(
    make,
    tokens,
    modality,
    token_mask,
    cotangent,
    mask_vector,
    ln_one_gain,
    ln_one_shift,
    w_qkv,
    w_out,
    ln_two_gain,
    ln_two_shift,
    w_up,
    w_down,
):
    net = make()
    part = w_qkv.shape[0]
    seqs = tokens.shape[0] // LEN
    rows = seqs * SEQ
    columns = jnp.stack([ln_one_gain, ln_one_shift, ln_two_gain, ln_two_shift], 1)
    packed = jnp.concatenate([w_qkv, w_out, jnp.pad(columns, ((0, 0), (0, 124)))], 1)
    n_columns = packed.shape[1]
    ring = net.turns(packed)

    seq_masks = token_mask.reshape(seqs, LEN)
    masked = jnp.concatenate(
        [
            jnp.pad(seq_masks[:, :PATCHES], ((0, 0), (0, HEAD - PATCHES))),
            jnp.pad(seq_masks[:, PATCHES:], ((0, 0), (0, TAIL - LEN + PATCHES))),
        ],
        1,
    ).reshape(1, rows)
    order = jnp.cumsum(masked, 1)
    place = jnp.where(masked == 1, order - 1, -1)
    blocks = jnp.maximum((order[0, rows - 1] + BLK - 1) // BLK, 1)
    near = jnp.arange(8, dtype=jnp.int32)
    near = jnp.bitwise_xor(net.flat, near & 3) * 2 + jnp.bitwise_xor(net.core, near >> 2)
    where_ref = jnp.concatenate(
        [
            near,
            jnp.stack([net.core, net.flat, blocks]).astype(jnp.int32),
            modality.reshape(seqs, LEN)[:, 0],
        ]
    )
    tokens = lay(tokens, seqs)
    ring, where_ref, tokens = tie(ring, where_ref, tokens)

    own = net.ring(ring, part)
    near = net.square(own)
    text, _ = tie(pack_expert(w_up[1], w_down[1]), own)
    ring_text = net.turns(text)
    masked = masked.astype(F32).reshape(rows, 1)
    cotangent = lay(cotangent, seqs)
    vector = mask_vector.astype(F32).reshape(1, D)
    near, masked, place, cotangent, vector = tie(near, masked, place, cotangent, vector)
    pieces = net.square_cores(near)
    own_text = net.ring(ring_text, part)
    pieces, own_text, image = tie(pieces, own_text, pack_expert(w_up[0], w_down[0]))
    near_text = net.sides(own_text)
    image = net.turns(image)

    qkv, softs, context, normed_one, params = call(
        attention_kernel,
        seqs,
        (where_ref, tokens, masked, vector, *pieces),
        [by_step((SEQ, D)), by_step((SEQ, 1)), whole((1, D))] + [ANY] * 8,
        [
            ((rows, 3 * D), BF16),
            ((seqs, H // 2, SEQ, 2 * SEQ), F32),
            ((rows, D), BF16),
            ((rows, D), BF16),
            ((8, D), F32),
        ],
        [
            by_step((SEQ, 3 * D)),
            by_step((1, H // 2, SEQ, 2 * SEQ)),
            by_step((SEQ, D)),
            by_step((SEQ, D)),
            pl.BlockSpec((8, D), lambda i, *_: (0, 0)),
        ],
        [pltpu.VMEM((D, n_columns), BF16), pltpu.SemaphoreType.DMA((10,))],
        "attention",
    )

    near_text, image, qkv, softs, context, normed_one, params = tie(
        near_text, image, qkv, softs, context, normed_one, params
    )
    near_text = net.corner(near_text)
    last, image = tie(net.last(near_text), net.ring(image, part))
    pieces_text = net.cores_of(near_text, last)
    image, pieces_text = tie(image, pieces_text)
    near_image = net.sides(image)

    block = (ROWS_ONE, D)
    keep, send, send_far, grad_context, sums = call(
        feed_back_kernel,
        4,
        (where_ref, place, vector, cotangent, context, params, *pieces_text, *pieces),
        [whole((1, rows)), whole((1, D)), whole((rows, D)), whole((rows, D)), whole((8, D))]
        + [ANY] * 18,
        [((4, *block), BF16), ((3, *block), BF16), (block, BF16), ((rows, D), BF16), ((8, D), F32)],
        [ANY] * 3 + [whole((rows, D)), whole((8, D))],
        [
            pltpu.VMEM((rows, D), BF16),
            pltpu.VMEM((rows, D), F32),
            pltpu.VMEM((rows, D), BF16),
            pltpu.VMEM((rows, D), BF16),
            pltpu.VMEM((rows, D), F32),
        ]
        + [pltpu.VMEM((D, D), F32)] * 2
        + [
            pltpu.VMEM((4, D, D), BF16),
            pltpu.VMEM((FF, D), BF16),
            pltpu.VMEM((D, D), BF16),
            pltpu.VMEM((2, 4, *block), BF16),
            pltpu.SemaphoreType.DMA((40,)),
            pltpu.SemaphoreType.DMA((10,)),
            pltpu.SemaphoreType.DMA((5, 5)),
        ],
        "feed_back",
    )
    near_image, keep, send, send_far, grad_context, sums = tie(
        near_image, keep, send, send_far, grad_context, sums
    )
    far = net.far_sums(keep, net.to_core(send_far))
    halves_image = net.halves(near_image)
    far, send, context, halves_image = tie(far, send, context, halves_image)
    got = net.to_core(send)
    corner = net.to_corner(far)
    near_image = net.to_corners(near_image, halves_image)
    experts = [pltpu.VMEM((4, D, D), BF16), pltpu.VMEM((FF, D), BF16)]
    after, normed_two = call(
        feed_text_kernel,
        4,
        (where_ref, tokens, masked, vector, context, params, *pieces_text, *pieces),
        [whole((rows, D)), whole((rows, 1)), whole((1, D)), whole((rows, D)), whole((8, D))]
        + [ANY] * 18,
        [((rows, D), F32), ((rows, D), BF16)],
        [whole((rows, D))] * 2,
        experts
        + [
            pltpu.VMEM((D, D), BF16),
            pltpu.SemaphoreType.DMA((40,)),
            pltpu.SemaphoreType.DMA((10,)),
            pltpu.VMEM((seqs * TAIL, D), BF16),
        ],
        "feed_text",
    )
    corner, got, near_image, after = tie(corner, got, near_image, after)
    sums_feed = net.side_sums(keep, got, corner)
    last_image = net.far_cores(net.last(near_image))
    sums_feed, grad_context, last_image = tie(sums_feed, grad_context, last_image)
    sums_feed = net.to_sides(sums_feed)
    far_image = net.far_cores(near_image[:3])

    keep, send, grad_tokens = call(
        attention_back_kernel,
        seqs,
        (where_ref, qkv, softs, grad_context, normed_one, tokens, masked, vector, params, sums)
        + tuple(pieces),
        [
            by_step((SEQ, 3 * D)),
            by_step((1, H // 2, SEQ, 2 * SEQ)),
            by_step((SEQ, D)),
            whole((rows, D)),
            by_step((SEQ, D)),
            by_step((SEQ, 1)),
            whole((1, D)),
            whole((8, D)),
            whole((8, D)),
        ]
        + [ANY] * 8,
        [((4, ROWS_QKV, D), BF16), ((4, ROWS_QKV, D), BF16), ((seqs * LEN, D), F32)],
        [ANY, ANY, whole((seqs * LEN, D))],
        [
            pltpu.VMEM((D, 3 * D), BF16),
            pltpu.VMEM((8, D), F32),
            pltpu.VMEM((rows, 3 * D), BF16),
            pltpu.VMEM((8, ROWS_QKV, D), BF16),
            pltpu.SemaphoreType.DMA((10,)),
            pltpu.SemaphoreType.DMA((8,)),
        ],
        "attention_back",
    )
    keep, send, grad_tokens, sums_feed, far_image = tie(
        keep, send, grad_tokens, sums_feed, far_image
    )
    got = net.to_core(send)
    pieces_image = net.all_cores(near_image, far_image, last_image)
    sums_qkv = net.plane_sums(keep, got, 296)
    ring_one = net.ring_sums(sums_feed, [(4, 96), (1, 384), (1, 96)])
    sums_qkv, ring_one, after, pieces_image = tie(sums_qkv, ring_one, after, pieces_image)
    sums_qkv = net.to_plane(sums_qkv)
    ring_one = net.to_ring(ring_one, (1, 2))
    (output,) = call(
        feed_image_kernel,
        4,
        (where_ref, normed_two, after, *pieces_image),
        [whole((rows, D)), whole((rows, D))] + [ANY] * 10,
        [((seqs * LEN, D), BF16)],
        [whole((seqs * LEN, D))],
        [pltpu.VMEM((rows, D), F32)]
        + experts
        + [pltpu.SemaphoreType.DMA((40,)), pltpu.VMEM((seqs * LEN, D), F32)],
        "feed_image",
    )
    sums_qkv, ring_one, output = tie(sums_qkv, ring_one, output)
    ring_two = net.ring_sums(sums_qkv, [(3, 96), (0, 8)])
    ring_one = net.to_ring(ring_one, (3,))
    ring_two = net.to_ring(ring_two, (1, 2, 3))

    grads = net.add_ring(ring_one)
    grad_w_up = grads[: 4 * part].reshape(4, part, D).transpose(1, 0, 2).reshape(part, FF)
    grad_w_down = grads[4 * part : 8 * part]
    grad_w_out = grads[8 * part : 9 * part]
    grads = net.add_ring(ring_two)
    grad_w_qkv = grads[: 3 * part].reshape(3, part, D).transpose(1, 0, 2).reshape(part, 3 * D)
    extra = grads[3 * part :]
    owned = lax.dynamic_slice_in_dim(extra, net.index * part, part, 1)

    return (
        output,
        grad_tokens,
        extra[2],
        owned[3],
        owned[4],
        grad_w_qkv,
        grad_w_out,
        owned[0],
        owned[1],
        grad_w_up,
        grad_w_down,
    )


def solution(mesh):
    if (mesh.shape["dp"], mesh.shape["fsdp"]) == (8, 4):
        mesh = Mesh(mesh.devices.reshape(2, 2, 2, 4), Cube.axes)
        make = Cube
    else:
        make = functools.partial(Flat, mesh.size)
    axes = Cube.axes if make is Cube else Flat.axes
    row, flat = P(axes, None), P(axes)
    middle = P(None, axes, None)
    in_specs = (row, flat, flat, row, P(), flat, flat, row, row, flat, flat, middle, middle)
    out_specs = (row, row, P(), flat, flat, row, row, flat, flat, row, row)
    return jax.shard_map(
        functools.partial(layer, make),
        mesh=mesh,
        in_specs=in_specs,
        out_specs=out_specs,
        check_vma=False,
    )
```

profile of v0, /device:TPU:16, one launch (start us, length us, event | category | flops | bytes accessed | tf_op | source)
XLA Modules:
  0.0 284.3 jit_solution(4720252679315965113)
XLA Ops:
  2.4 1.6 collective-permute-start
  4.4 1.2 collective-permute-start.2
  10.7 1.8 reshape.311
  12.5 1.8 reshape.314
  14.3 1.7 slice_select_fusion
  16.6 2.6 fusion.5
  20.4 1.7 collective-permute-start.3
  23.0 1.5 collective-permute-start.4
  26.5 2.6 collective-permute-start.11
  29.0 8.3 %collective-permute-done.3.rest_1_.rest_11_ = bf16[96,3200]{1,0:T(8,128)(2,1)S(1)} collective-permute-done((bf16[96,3200]{1,0:T(8,128)(2,1)S(1)}, bf16[96,3200]{1,0:T(8,128)(2,1)S(1)}, u32[]{:S(2)}, u32[]{:S(2)}) %collective-permute-start.3) | collective-permute-done | bytes 614432 | tf_op jit(solution)/shard_map/ppermute | solution.py:561
  37.3 1.9 collective-permute-start.12
  40.7 1.6 pad_maximum_fusion.10
  42.4 2.5 fusion.6
  44.9 5.8 %collective-permute-done.4.rest_2_.rest_12_ = bf16[96,3200]{1,0:T(8,128)(2,1)S(1)} collective-permute-done((bf16[96,3200]{1,0:T(8,128)(2,1)S(1)}, bf16[96,3200]{1,0:T(8,128)(2,1)S(1)}, u32[]{:S(2)}, u32[]{:S(2)}) %collective-permute-start.4) | collective-permute-done | bytes 614432 | tf_op jit(solution)/shard_map/ppermute | solution.py:561
  53.0 1.4 select_bitcast_fusion.7
  55.6 1.1 collective-permute-start.13
  56.8 1.5 collective-permute-start.14
  59.4 2.9 %collective-permute-start.16 = (bf16[192,768]{1,0:T(8,128)(2,1)}, bf16[192,768]{1,0:T(8,128)(2,1)S(1)}, u32[]{:S(2)}, u32[]{:S(2)}) collective-permute-start(bf16[192,768]{1,0:T(8,128)(2,1)} %pad_maximum_fusion.10), channel_id=1, source_target_pairs={{0,2},{1,3},{2,0},{3,1},{4,6},{5,7},{6,4},{7,5},{8,10},{9,11},{10,... | collective-permute-start | bytes 884744 | tf_op jit(solution)/shard_map/ppermute | solution.py:542
  62.2 1.6 collective-permute-start.17
  64.9 22.6 %attention.1 = (bf16[1024,2304]{1,0:T(8,128)(2,1)}, f32[4,6,256,512]{3,2,1,0:T(8,128)}, bf16[1024,768]{1,0:T(8,128)(2,1)}, bf16[1024,768]{1,0:T(8,128)(2,1)}, f32[8,768]{1,0:T(8,128)}) custom-call(s32[15]{0:T(128)} %concatenate.53.where_ref, bf16[1024,768]{1,0:T(8,128)(2,1)} %bitcast.150, f32[1024,1]{1,0:T(8,128)} %copy.45.masked, ...), custom_call_target="tpu_custom_call" | custom-call | flops 1 | bytes 1 | tf_op jit(solution)/shard_map/attention/pallas_call | solution.py:502
  88.6 1.2 slice.211
  90.7 1.1 collective-permute-start.19
  94.4 11.1 %collective-permute-done.18.rest_3_ = bf16[384,768]{1,0:T(8,128)(2,1)S(1)} collective-permute-done((bf16[384,768]{1,0:T(8,128)(2,1)S(1)}, bf16[384,768]{1,0:T(8,128)(2,1)S(1)}, u32[]{:S(2)}, u32[]{:S(2)}) %collective-permute-start.18) | collective-permute-done | bytes 589856 | tf_op jit(solution)/shard_map/ppermute | solution.py:561
  108.6 1.1 collective-permute-start.25
  109.8 1.5 collective-permute-start.26
  111.3 21.8 %feed_back.1 = (bf16[4,864,768]{2,1,0:T(8,128)(2,1)}, bf16[3,864,768]{2,1,0:T(8,128)(2,1)}, bf16[864,768]{1,0:T(8,128)(2,1)}, bf16[1024,768]{1,0:T(8,128)(2,1)}, f32[8,768]{1,0:T(8,128)}) custom-call(s32[15]{0:T(128)} %concatenate.53.where_ref, s32[1,1024]{1,0:T(1,128)} %get-tuple-element.188.place, f32[1,768]{1,0:T(1,128)} %reshape.355.vector, ...), custom_call_target="tpu_custom_call" | custom-call | flops 1 | bytes 1 | tf_op jit(solution)/shard_map/feed_back/pallas_call | solution.py:502
  133.1 3.9 %collective-permute-done.25.rest_1_ = bf16[768,768]{1,0:T(8,128)(2,1)} collective-permute-done((bf16[768,768]{1,0:T(8,128)(2,1)}, bf16[768,768]{1,0:T(8,128)(2,1)}, u32[]{:S(2)}, u32[]{:S(2)}) %collective-permute-start.25) | collective-permute-done | bytes 1179680 | tf_op jit(solution)/shard_map/ppermute | solution.py:561
  137.8 1.9 slice.218
  139.8 2.0 slice.219
  141.7 2.7 fusion.7
  144.9 1.1 collective-permute-start.28
  146.1 7.4 %collective-permute-start.29 = (bf16[432,768]{1,0:T(8,128)(2,1)}, bf16[432,768]{1,0:T(8,128)(2,1)}, u32[]{:S(2)}, u32[]{:S(2)}) collective-permute-start(bf16[432,768]{1,0:T(8,128)(2,1)} %get-tuple-element.213), channel_id=1, source_target_pairs={{0,16},{16,0},{1,17},{17,1},{2,18},{18,2},{3,19},{19,3},{4,20},{20... | collective-permute-start | bytes 1990664 | tf_op jit(solution)/shard_map/ppermute | solution.py:561
  153.5 14.0 %feed_text.1 = (f32[1024,768]{1,0:T(8,128)}, bf16[1024,768]{1,0:T(8,128)(2,1)}) custom-call(s32[15]{0:T(128)} %concatenate.53.where_ref, bf16[1024,768]{1,0:T(8,128)(2,1)} %bitcast.151, f32[1024,1]{1,0:T(8,128)} %copy.45.masked, f32[1,768]{1,0:T(1,128)} %reshape.355.vector, bf16[1024,768]{1,0:T(8,128)(2,1)} %get-tuple-element.218.context, ...), custom_call_target="tpu_custom_call" | custom-call | flops 1 | bytes 1 | tf_op jit(solution)/shard_map/feed_text/pallas_call | solution.py:502
  167.5 13.7 %collective-permute-done.31.rest_3_ = bf16[384,768]{1,0:T(8,128)(2,1)} collective-permute-done((bf16[384,768]{1,0:T(8,128)(2,1)}, bf16[384,768]{1,0:T(8,128)(2,1)}, u32[]{:S(2)}, u32[]{:S(2)}) %collective-permute-start.31) | collective-permute-done | bytes 589856 | tf_op jit(solution)/shard_map/ppermute | solution.py:561
  181.8 5.2 %fusion.3 = (bf16[864,768]{1,0:T(8,128)(2,1)}, bf16[864,768]{1,0:T(8,128)(2,1)}) fusion(bf16[432,768]{1,0:T(8,128)(2,1)} %collective-permute-done.28, bf16[3,864,768]{2,1,0:T(8,128)(2,1)S(1)} %collective-permute-done.30, bf16[4,864,768]{2,1,0:T(8,128)(2,1)} %get-tuple-element.241, bf16[432,768]{1,0:T(8,128)(2,1)} %collective-permute-done.29), kind=kLoop, calls=%fused_computation.6 | loop fusion | flops 7962624 | bytes 9289728 | tf_op jit(solution)/shard_map/convert_element_type | solution.py:605
  188.2 1.7 collective-permute-start.36
  190.4 30.5 %attention_back.1 = (bf16[4,304,768]{2,1,0:T(8,128)(2,1)}, bf16[4,304,768]{2,1,0:T(8,128)(2,1)}, f32[948,768]{1,0:T(8,128)}) custom-call(s32[15]{0:T(128)} %concatenate.53.where_ref, bf16[1024,2304]{1,0:T(8,128)(2,1)} %get-tuple-element.175.qkv, f32[4,6,256,512]{3,2,1,0:T(8,128)} %get-tuple-element.176.softs, ...), custom_call_target="tpu_custom_call" | custom-call | flops 1 | bytes 1 | tf_op jit(solution)/shard_map/attention_back/pallas_call | solution.py:502
  221.5 2.4 fusion.18
  226.9 1.6 fusion.13
  228.5 1.7 collective-permute-start.41
  230.5 1.5 collective-permute-start.43
  232.0 22.0 %feed_image.1 = bf16[948,768]{1,0:T(8,128)(2,1)} custom-call(s32[15]{0:T(128)} %concatenate.53.where_ref, bf16[1024,768]{1,0:T(8,128)(2,1)} %get-tuple-element.260.rows_in, f32[1024,768]{1,0:T(8,128)} %get-tuple-element.261.before, bf16[768,768]{1,0:T(8,128)(2,1)} %pad_maximum_fusion.3.rest_0_, bf16[768,768]{1,0:T(8,128)(2,1)} %collective-permute-done.25.rest_1_, ...), custom_call_target="tpu_custom_call" | custom-call | flops 1 | bytes 1 | tf_op jit(solution)/shard_map/feed_image/pallas_call | solution.py:502
  254.9 1.6 fusion.16
  257.5 4.3 %collective-permute-start.47 = (bf16[80,768]{1,0:T(8,128)(2,1)S(1)}, bf16[80,768]{1,0:T(8,128)(2,1)S(1)}, u32[]{:S(2)}, u32[]{:S(2)}) collective-permute-start(bf16[80,768]{1,0:T(8,128)(2,1)S(1)} %get-tuple-element.337), channel_id=1, source_target_pairs={{0,2},{1,3},{2,0},{3,1},{4,6},{5,7},{6,4},{7,5},{8,10},{9,11},{10,... | collective-permute-start | bytes 368648 | tf_op jit(solution)/shard_map/ppermute | solution.py:542
  261.9 2.1 collective-permute-start.49
  264.0 5.2 %collective-permute-done.47 = bf16[80,768]{1,0:T(8,128)(2,1)S(1)} collective-permute-done((bf16[80,768]{1,0:T(8,128)(2,1)S(1)}, bf16[80,768]{1,0:T(8,128)(2,1)S(1)}, u32[]{:S(2)}, u32[]{:S(2)}) %collective-permute-start.47) | collective-permute-done | bytes 122912 | tf_op jit(solution)/shard_map/ppermute | solution.py:542
  269.2 9.3 %collective-permute-done.46 = bf16[80,768]{1,0:T(8,128)(2,1)S(1)} collective-permute-done((bf16[80,768]{1,0:T(8,128)(2,1)S(1)}, bf16[80,768]{1,0:T(8,128)(2,1)S(1)}, u32[]{:S(2)}, u32[]{:S(2)}) %collective-permute-start.46) | collective-permute-done | bytes 122912 | tf_op jit(solution)/shard_map/ppermute | solution.py:542
  280.6 1.2 add_add_fusion
  (215 shorter events, 39.3 us)
Async XLA Ops:
  2.4 16.8 %collective-permute-start = (bf16[24,3200]{1,0:T(8,128)(2,1)S(1)}, bf16[24,3200]{1,0:T(8,128)(2,1)S(1)}, u32[]{:S(2)}, u32[]{:S(2)}) collective-permute-start(bf16[24,3200]{1,0:T(8,128)(2,1)S(1)} %fusion.15), channel_id=1, source_target_pairs={{0,1},{1,2},{2,3},{3,0},{4,5},{5,6},{6,7},{7,4},{8,9},{9,10},{10,1... | collective-permute-start | bytes 460808 | tf_op jit(solution)/shard_map/ppermute | solution.py:542
  4.0 15.1 %collective-permute-start.1 = (bf16[24,3200]{1,0:T(8,128)(2,1)S(1)}, bf16[24,3200]{1,0:T(8,128)(2,1)}, u32[]{:S(2)}, u32[]{:S(2)}) collective-permute-start(bf16[24,3200]{1,0:T(8,128)(2,1)S(1)} %fusion.15), channel_id=1, source_target_pairs={{0,2},{1,3},{2,0},{3,1},{4,6},{5,7},{6,4},{7,5},{8,10},{9,11},{10,... | collective-permute-start | bytes 460808 | tf_op jit(solution)/shard_map/ppermute | solution.py:542
  4.4 14.8 %collective-permute-start.2 = (bf16[24,3200]{1,0:T(8,128)(2,1)S(1)}, bf16[24,3200]{1,0:T(8,128)(2,1)}, u32[]{:S(2)}, u32[]{:S(2)}) collective-permute-start(bf16[24,3200]{1,0:T(8,128)(2,1)S(1)} %fusion.15), channel_id=1, source_target_pairs={{0,3},{1,0},{2,1},{3,2},{4,7},{5,4},{6,5},{7,6},{8,11},{9,8},{10,9... | collective-permute-start | bytes 460808 | tf_op jit(solution)/shard_map/ppermute | solution.py:542
  20.4 16.9 %collective-permute-start.3 = (bf16[96,3200]{1,0:T(8,128)(2,1)S(1)}, bf16[96,3200]{1,0:T(8,128)(2,1)S(1)}, u32[]{:S(2)}, u32[]{:S(2)}) collective-permute-start(bf16[96,3200]{1,0:T(8,128)(2,1)S(1)} %bitcast.153), channel_id=1, source_target_pairs={{0,8},{8,0},{1,9},{9,1},{2,10},{10,2},{3,11},{11,3},{4,12},{12,4},... | collective-permute-start | bytes 1843208 | tf_op jit(solution)/shard_map/ppermute | solution.py:561
  23.0 27.8 %collective-permute-start.4 = (bf16[96,3200]{1,0:T(8,128)(2,1)S(1)}, bf16[96,3200]{1,0:T(8,128)(2,1)S(1)}, u32[]{:S(2)}, u32[]{:S(2)}) collective-permute-start(bf16[96,3200]{1,0:T(8,128)(2,1)S(1)} %bitcast.154), channel_id=1, source_target_pairs={{0,16},{16,0},{1,17},{17,1},{2,18},{18,2},{3,19},{19,3},{4,20},{20... | collective-permute-start | bytes 1843208 | tf_op jit(solution)/shard_map/ppermute | solution.py:561
  24.5 26.3 %collective-permute-start.5 = (bf16[96,3200]{1,0:T(8,128)(2,1)S(1)}, bf16[96,3200]{1,0:T(8,128)(2,1)}, u32[]{:S(2)}, u32[]{:S(2)}) collective-permute-start(bf16[96,3200]{1,0:T(8,128)(2,1)S(1)} %bitcast.155), channel_id=1, source_target_pairs={{0,24},{8,16},{16,8},{24,0},{1,25},{9,17},{17,9},{25,1},{2,26},{10... | collective-permute-start | bytes 1843208 | tf_op jit(solution)/shard_map/ppermute | solution.py:584
  25.8 25.6 %collective-permute-start.10 = (bf16[192,768]{1,0:T(8,128)(2,1)}, bf16[192,768]{1,0:T(8,128)(2,1)}, u32[]{:S(2)}, u32[]{:S(2)}) collective-permute-start(bf16[192,768]{1,0:T(8,128)(2,1)} %pad_maximum_fusion.9), channel_id=1, source_target_pairs={{0,1},{1,2},{2,3},{3,0},{4,5},{5,6},{6,7},{7,4},{8,9},{9,10},{10,1... | collective-permute-start | bytes 884744 | tf_op jit(solution)/shard_map/ppermute | solution.py:542
  26.5 25.0 %collective-permute-start.11 = (bf16[192,768]{1,0:T(8,128)(2,1)}, bf16[192,768]{1,0:T(8,128)(2,1)}, u32[]{:S(2)}, u32[]{:S(2)}) collective-permute-start(bf16[192,768]{1,0:T(8,128)(2,1)} %pad_maximum_fusion.9), channel_id=1, source_target_pairs={{0,2},{1,3},{2,0},{3,1},{4,6},{5,7},{6,4},{7,5},{8,10},{9,11},{10,... | collective-permute-start | bytes 884744 | tf_op jit(solution)/shard_map/ppermute | solution.py:542
  37.3 15.6 %collective-permute-start.12 = (bf16[192,768]{1,0:T(8,128)(2,1)}, bf16[192,768]{1,0:T(8,128)(2,1)}, u32[]{:S(2)}, u32[]{:S(2)}) collective-permute-start(bf16[192,768]{1,0:T(8,128)(2,1)} %pad_maximum_fusion.9), channel_id=1, source_target_pairs={{0,3},{1,0},{2,1},{3,2},{4,7},{5,4},{6,5},{7,6},{8,11},{9,8},{10,9... | collective-permute-start | bytes 884744 | tf_op jit(solution)/shard_map/ppermute | solution.py:542
  50.8 4.0 %collective-permute-start.6 = (bf16[96,3200]{1,0:T(8,128)(2,1)S(1)}, bf16[96,3200]{1,0:T(8,128)(2,1)S(1)}, u32[]{:S(2)}, u32[]{:S(2)}) collective-permute-start(bf16[96,3200]{1,0:T(8,128)(2,1)S(1)} %bitcast.156), channel_id=1, source_target_pairs={{0,4},{4,0},{1,5},{5,1},{2,6},{6,2},{3,7},{7,3},{8,12},{12,8},{9,1... | collective-permute-start | bytes 1843208 | tf_op jit(solution)/shard_map/ppermute | solution.py:561
  50.9 3.9 %collective-permute-start.7 = (bf16[96,3200]{1,0:T(8,128)(2,1)S(1)}, bf16[96,3200]{1,0:T(8,128)(2,1)S(1)}, u32[]{:S(2)}, u32[]{:S(2)}) collective-permute-start(bf16[96,3200]{1,0:T(8,128)(2,1)S(1)} %collective-permute-done.3.rest_1_.rest_11_), channel_id=1, source_target_pairs={{0,4},{4,0},{1,5},{5,1},{2,6},{6,2},{3,7},{7,3},{8,12},{12,8},{9,1... | collective-permute-start | bytes 1843208 | tf_op jit(solution)/shard_map/ppermute | solution.py:561
  51.3 4.2 %collective-permute-start.8 = (bf16[96,3200]{1,0:T(8,128)(2,1)S(1)}, bf16[96,3200]{1,0:T(8,128)(2,1)S(1)}, u32[]{:S(2)}, u32[]{:S(2)}) collective-permute-start(bf16[96,3200]{1,0:T(8,128)(2,1)S(1)} %collective-permute-done.4.rest_2_.rest_12_), channel_id=1, source_target_pairs={{0,4},{4,0},{1,5},{5,1},{2,6},{6,2},{3,7},{7,3},{8,12},{12,8},{9,1... | collective-permute-start | bytes 1843208 | tf_op jit(solution)/shard_map/ppermute | solution.py:561
  51.4 4.1 %collective-permute-start.9 = (bf16[96,3200]{1,0:T(8,128)(2,1)}, bf16[96,3200]{1,0:T(8,128)(2,1)S(1)}, u32[]{:S(2)}, u32[]{:S(2)}) collective-permute-start(bf16[96,3200]{1,0:T(8,128)(2,1)} %collective-permute-done.5.rest_3_.rest_13_), channel_id=1, source_target_pairs={{0,4},{4,0},{1,5},{5,1},{2,6},{6,2},{3,7},{7,3},{8,12},{12,8},{9,1... | collective-permute-start | bytes 1843208 | tf_op jit(solution)/shard_map/ppermute | solution.py:561
  55.6 31.9 %collective-permute-start.13 = (bf16[768,768]{1,0:T(8,128)(2,1)S(1)}, bf16[768,768]{1,0:T(8,128)(2,1)S(1)}, u32[]{:S(2)}, u32[]{:S(2)}) collective-permute-start(bf16[768,768]{1,0:T(8,128)(2,1)S(1)} %pad_maximum_fusion.1.rest_0_), channel_id=1, source_target_pairs={{0,8},{8,0},{1,9},{9,1},{2,10},{10,2},{3,11},{11,3},{4,12},{12,4},... | collective-permute-start | bytes 3538952 | tf_op jit(solution)/shard_map/ppermute | solution.py:561
  56.8 30.8 %collective-permute-start.14 = (bf16[768,768]{1,0:T(8,128)(2,1)S(1)}, bf16[768,768]{1,0:T(8,128)(2,1)}, u32[]{:S(2)}, u32[]{:S(2)}) collective-permute-start(bf16[768,768]{1,0:T(8,128)(2,1)S(1)} %pad_maximum_fusion.1.rest_0_), channel_id=1, source_target_pairs={{0,16},{16,0},{1,17},{17,1},{2,18},{18,2},{3,19},{19,3},{4,20},{20... | collective-permute-start | bytes 3538952 | tf_op jit(solution)/shard_map/ppermute | solution.py:561
  58.3 29.2 %collective-permute-start.15 = (bf16[192,768]{1,0:T(8,128)(2,1)}, bf16[192,768]{1,0:T(8,128)(2,1)S(1)}, u32[]{:S(2)}, u32[]{:S(2)}) collective-permute-start(bf16[192,768]{1,0:T(8,128)(2,1)} %pad_maximum_fusion.10), channel_id=1, source_target_pairs={{0,1},{1,2},{2,3},{3,0},{4,5},{5,6},{6,7},{7,4},{8,9},{9,10},{10,1... | collective-permute-start | bytes 884744 | tf_op jit(solution)/shard_map/ppermute | solution.py:542
  59.4 28.2 %collective-permute-start.16 = (bf16[192,768]{1,0:T(8,128)(2,1)}, bf16[192,768]{1,0:T(8,128)(2,1)S(1)}, u32[]{:S(2)}, u32[]{:S(2)}) collective-permute-start(bf16[192,768]{1,0:T(8,128)(2,1)} %pad_maximum_fusion.10), channel_id=1, source_target_pairs={{0,2},{1,3},{2,0},{3,1},{4,6},{5,7},{6,4},{7,5},{8,10},{9,11},{10,... | collective-permute-start | bytes 884744 | tf_op jit(solution)/shard_map/ppermute | solution.py:542
  62.2 25.3 %collective-permute-start.17 = (bf16[192,768]{1,0:T(8,128)(2,1)}, bf16[192,768]{1,0:T(8,128)(2,1)S(1)}, u32[]{:S(2)}, u32[]{:S(2)}) collective-permute-start(bf16[192,768]{1,0:T(8,128)(2,1)} %pad_maximum_fusion.10), channel_id=1, source_target_pairs={{0,3},{1,0},{2,1},{3,2},{4,7},{5,4},{6,5},{7,6},{8,11},{9,8},{10,9... | collective-permute-start | bytes 884744 | tf_op jit(solution)/shard_map/ppermute | solution.py:542
  88.5 17.8 %collective-permute-start.21 = (bf16[768,768]{1,0:T(8,128)(2,1)S(1)}, bf16[768,768]{1,0:T(8,128)(2,1)S(1)}, u32[]{:S(2)}, u32[]{:S(2)}) collective-permute-start(bf16[768,768]{1,0:T(8,128)(2,1)S(1)} %collective-permute-done.13.rest_1_), channel_id=1, source_target_pairs={{0,4},{4,0},{1,5},{5,1},{2,6},{6,2},{3,7},{7,3},{8,12},{12,8},{9,1... | collective-permute-start | bytes 3538952 | tf_op jit(solution)/shard_map/ppermute | solution.py:561
  89.7 17.6 %collective-permute-start.22 = (bf16[768,768]{1,0:T(8,128)(2,1)}, bf16[768,768]{1,0:T(8,128)(2,1)}, u32[]{:S(2)}, u32[]{:S(2)}) collective-permute-start(bf16[768,768]{1,0:T(8,128)(2,1)} %collective-permute-done.14.rest_2_), channel_id=1, source_target_pairs={{0,4},{4,0},{1,5},{5,1},{2,6},{6,2},{3,7},{7,3},{8,12},{12,8},{9,1... | collective-permute-start | bytes 3538952 | tf_op jit(solution)/shard_map/ppermute | solution.py:561
  90.2 15.3 %collective-permute-start.18 = (bf16[384,768]{1,0:T(8,128)(2,1)S(1)}, bf16[384,768]{1,0:T(8,128)(2,1)S(1)}, u32[]{:S(2)}, u32[]{:S(2)}) collective-permute-start(bf16[384,768]{1,0:T(8,128)(2,1)S(1)} %slice.210), channel_id=1, source_target_pairs={{0,16},{16,0},{1,17},{17,1},{2,18},{18,2},{3,19},{19,3},{4,20},{20... | collective-permute-start | bytes 1769480 | tf_op jit(solution)/shard_map/ppermute | solution.py:561
  90.7 15.0 %collective-permute-start.19 = (bf16[384,768]{1,0:T(8,128)(2,1)S(1)}, bf16[384,768]{1,0:T(8,128)(2,1)S(1)}, u32[]{:S(2)}, u32[]{:S(2)}) collective-permute-start(bf16[384,768]{1,0:T(8,128)(2,1)S(1)} %slice.211), channel_id=1, source_target_pairs={{0,8},{8,0},{1,9},{9,1},{2,10},{10,2},{3,11},{11,3},{4,12},{12,4},... | collective-permute-start | bytes 1769480 | tf_op jit(solution)/shard_map/ppermute | solution.py:561
  91.9 14.4 %collective-permute-start.20 = (bf16[768,768]{1,0:T(8,128)(2,1)S(1)}, bf16[768,768]{1,0:T(8,128)(2,1)S(1)}, u32[]{:S(2)}, u32[]{:S(2)}) collective-permute-start(bf16[768,768]{1,0:T(8,128)(2,1)S(1)} %pad_maximum_fusion.1.rest_0_), channel_id=1, source_target_pairs={{0,4},{4,0},{1,5},{5,1},{2,6},{6,2},{3,7},{7,3},{8,12},{12,8},{9,1... | collective-permute-start | bytes 3538952 | tf_op jit(solution)/shard_map/ppermute | solution.py:561
  108.6 28.3 %collective-permute-start.25 = (bf16[768,768]{1,0:T(8,128)(2,1)}, bf16[768,768]{1,0:T(8,128)(2,1)}, u32[]{:S(2)}, u32[]{:S(2)}) collective-permute-start(bf16[768,768]{1,0:T(8,128)(2,1)} %pad_maximum_fusion.3.rest_0_), channel_id=1, source_target_pairs={{0,8},{8,0},{1,9},{9,1},{2,10},{10,2},{3,11},{11,3},{4,12},{12,4},... | collective-permute-start | bytes 3538952 | tf_op jit(solution)/shard_map/ppermute | solution.py:561
  109.8 28.1 %collective-permute-start.26 = (bf16[768,768]{1,0:T(8,128)(2,1)}, bf16[768,768]{1,0:T(8,128)(2,1)}, u32[]{:S(2)}, u32[]{:S(2)}) collective-permute-start(bf16[768,768]{1,0:T(8,128)(2,1)} %pad_maximum_fusion.3.rest_0_), channel_id=1, source_target_pairs={{0,16},{16,0},{1,17},{17,1},{2,18},{18,2},{3,19},{19,3},{4,20},{20... | collective-permute-start | bytes 3538952 | tf_op jit(solution)/shard_map/ppermute | solution.py:561
  137.8 3.9 %collective-permute-start.27 = (bf16[864,768]{1,0:T(8,128)(2,1)}, bf16[864,768]{1,0:T(8,128)(2,1)S(1)}, u32[]{:S(2)}, u32[]{:S(2)}) collective-permute-start(bf16[864,768]{1,0:T(8,128)(2,1)} %get-tuple-element.208), channel_id=1, source_target_pairs={{0,4},{4,0},{1,5},{5,1},{2,6},{6,2},{3,7},{7,3},{8,12},{12,8},{9,1... | collective-permute-start | bytes 3981320 | tf_op jit(solution)/shard_map/ppermute | solution.py:561
  144.4 36.8 %collective-permute-start.30 = (bf16[3,864,768]{2,1,0:T(8,128)(2,1)}, bf16[3,864,768]{2,1,0:T(8,128)(2,1)S(1)}, u32[]{:S(2)}, u32[]{:S(2)}) collective-permute-start(bf16[3,864,768]{2,1,0:T(8,128)(2,1)} %get-tuple-element.214), channel_id=1, source_target_pairs={{0,4},{4,0},{1,5},{5,1},{2,6},{6,2},{3,7},{7,3},{8,12},{12,8},{9,1... | collective-permute-start | bytes 11943944 | tf_op jit(solution)/shard_map/ppermute | solution.py:561
  144.9 36.3 %collective-permute-start.28 = (bf16[432,768]{1,0:T(8,128)(2,1)}, bf16[432,768]{1,0:T(8,128)(2,1)}, u32[]{:S(2)}, u32[]{:S(2)}) collective-permute-start(bf16[432,768]{1,0:T(8,128)(2,1)} %get-tuple-element.212), channel_id=1, source_target_pairs={{0,8},{8,0},{1,9},{9,1},{2,10},{10,2},{3,11},{11,3},{4,12},{12,4},... | collective-permute-start | bytes 1990664 | tf_op jit(solution)/shard_map/ppermute | solution.py:561
  146.1 35.1 %collective-permute-start.29 = (bf16[432,768]{1,0:T(8,128)(2,1)}, bf16[432,768]{1,0:T(8,128)(2,1)}, u32[]{:S(2)}, u32[]{:S(2)}) collective-permute-start(bf16[432,768]{1,0:T(8,128)(2,1)} %get-tuple-element.213), channel_id=1, source_target_pairs={{0,16},{16,0},{1,17},{17,1},{2,18},{18,2},{3,19},{19,3},{4,20},{20... | collective-permute-start | bytes 1990664 | tf_op jit(solution)/shard_map/ppermute | solution.py:561
  153.4 27.8 %collective-permute-start.31 = (bf16[384,768]{1,0:T(8,128)(2,1)}, bf16[384,768]{1,0:T(8,128)(2,1)}, u32[]{:S(2)}, u32[]{:S(2)}) collective-permute-start(bf16[384,768]{1,0:T(8,128)(2,1)} %slice.218), channel_id=1, source_target_pairs={{0,16},{16,0},{1,17},{17,1},{2,18},{18,2},{3,19},{19,3},{4,20},{20... | collective-permute-start | bytes 1769480 | tf_op jit(solution)/shard_map/ppermute | solution.py:561
  153.5 27.7 %collective-permute-start.32 = (bf16[384,768]{1,0:T(8,128)(2,1)}, bf16[384,768]{1,0:T(8,128)(2,1)}, u32[]{:S(2)}, u32[]{:S(2)}) collective-permute-start(bf16[384,768]{1,0:T(8,128)(2,1)} %slice.219), channel_id=1, source_target_pairs={{0,8},{8,0},{1,9},{9,1},{2,10},{10,2},{3,11},{11,3},{4,12},{12,4},... | collective-permute-start | bytes 1769480 | tf_op jit(solution)/shard_map/ppermute | solution.py:561
  181.2 5.8 %collective-permute-start.33 = (bf16[384,768]{1,0:T(8,128)(2,1)}, bf16[384,768]{1,0:T(8,128)(2,1)S(1)}, u32[]{:S(2)}, u32[]{:S(2)}) collective-permute-start(bf16[384,768]{1,0:T(8,128)(2,1)} %collective-permute-done.31.rest_3_), channel_id=1, source_target_pairs={{0,4},{4,0},{1,5},{5,1},{2,6},{6,2},{3,7},{7,3},{8,12},{12,8},{9,1... | collective-permute-start | bytes 1769480 | tf_op jit(solution)/shard_map/ppermute | solution.py:561
  181.3 5.7 %collective-permute-start.34 = (bf16[384,768]{1,0:T(8,128)(2,1)}, bf16[384,768]{1,0:T(8,128)(2,1)S(1)}, u32[]{:S(2)}, u32[]{:S(2)}) collective-permute-start(bf16[384,768]{1,0:T(8,128)(2,1)} %collective-permute-done.32.rest_4_), channel_id=1, source_target_pairs={{0,4},{4,0},{1,5},{5,1},{2,6},{6,2},{3,7},{7,3},{8,12},{12,8},{9,1... | collective-permute-start | bytes 1769480 | tf_op jit(solution)/shard_map/ppermute | solution.py:561
  187.8 33.1 %collective-permute-start.35 = (bf16[864,768]{1,0:T(8,128)(2,1)}, bf16[864,768]{1,0:T(8,128)(2,1)S(1)}, u32[]{:S(2)}, u32[]{:S(2)}) collective-permute-start(bf16[864,768]{1,0:T(8,128)(2,1)} %get-tuple-element.234), channel_id=1, source_target_pairs={{0,8},{8,0},{1,9},{9,1},{2,10},{10,2},{3,11},{11,3},{4,12},{12,4},... | collective-permute-start | bytes 3981320 | tf_op jit(solution)/shard_map/ppermute | solution.py:561
  188.2 32.8 %collective-permute-start.36 = (bf16[864,768]{1,0:T(8,128)(2,1)}, bf16[864,768]{1,0:T(8,128)(2,1)S(1)}, u32[]{:S(2)}, u32[]{:S(2)}) collective-permute-start(bf16[864,768]{1,0:T(8,128)(2,1)} %get-tuple-element.235), channel_id=1, source_target_pairs={{0,16},{16,0},{1,17},{17,1},{2,18},{18,2},{3,19},{19,3},{4,20},{20... | collective-permute-start | bytes 3981320 | tf_op jit(solution)/shard_map/ppermute | solution.py:561
  189.9 31.0 %collective-permute-start.37 = (bf16[768,768]{1,0:T(8,128)(2,1)}, bf16[768,768]{1,0:T(8,128)(2,1)}, u32[]{:S(2)}, u32[]{:S(2)}) collective-permute-start(bf16[768,768]{1,0:T(8,128)(2,1)} %pad_maximum_fusion.3.rest_0_), channel_id=1, source_target_pairs={{0,4},{4,0},{1,5},{5,1},{2,6},{6,2},{3,7},{7,3},{8,12},{12,8},{9,1... | collective-permute-start | bytes 3538952 | tf_op jit(solution)/shard_map/ppermute | solution.py:561
  189.9 31.0 %collective-permute-start.38 = (bf16[768,768]{1,0:T(8,128)(2,1)}, bf16[768,768]{1,0:T(8,128)(2,1)}, u32[]{:S(2)}, u32[]{:S(2)}) collective-permute-start(bf16[768,768]{1,0:T(8,128)(2,1)} %collective-permute-done.25.rest_1_), channel_id=1, source_target_pairs={{0,4},{4,0},{1,5},{5,1},{2,6},{6,2},{3,7},{7,3},{8,12},{12,8},{9,1... | collective-permute-start | bytes 3538952 | tf_op jit(solution)/shard_map/ppermute | solution.py:561
  190.4 30.5 %collective-permute-start.39 = (bf16[768,768]{1,0:T(8,128)(2,1)}, bf16[768,768]{1,0:T(8,128)(2,1)}, u32[]{:S(2)}, u32[]{:S(2)}) collective-permute-start(bf16[768,768]{1,0:T(8,128)(2,1)} %collective-permute-done.26.rest_2_), channel_id=1, source_target_pairs={{0,4},{4,0},{1,5},{5,1},{2,6},{6,2},{3,7},{7,3},{8,12},{12,8},{9,1... | collective-permute-start | bytes 3538952 | tf_op jit(solution)/shard_map/ppermute | solution.py:561
  221.0 5.1 %collective-permute-start.40 = (bf16[4,304,768]{2,1,0:T(8,128)(2,1)}, bf16[4,304,768]{2,1,0:T(8,128)(2,1)S(1)}, u32[]{:S(2)}, u32[]{:S(2)}) collective-permute-start(bf16[4,304,768]{2,1,0:T(8,128)(2,1)} %get-tuple-element.240), channel_id=1, source_target_pairs={{0,4},{4,0},{1,5},{5,1},{2,6},{6,2},{3,7},{7,3},{8,12},{12,8},{9,1... | collective-permute-start | bytes 5603336 | tf_op jit(solution)/shard_map/ppermute | solution.py:561
  228.5 25.6 %collective-permute-start.41 = (bf16[296,768]{1,0:T(8,128)(2,1)}, bf16[296,768]{1,0:T(8,128)(2,1)S(1)}, u32[]{:S(2)}, u32[]{:S(2)}) collective-permute-start(bf16[296,768]{1,0:T(8,128)(2,1)} %get-tuple-element.253), channel_id=1, source_target_pairs={{0,8},{8,0},{1,9},{9,1},{2,10},{10,2},{3,11},{11,3},{4,12},{12,4},... | collective-permute-start | bytes 1363976 | tf_op jit(solution)/shard_map/ppermute | solution.py:561
  230.2 23.9 %collective-permute-start.42 = (bf16[296,768]{1,0:T(8,128)(2,1)}, bf16[296,768]{1,0:T(8,128)(2,1)S(1)}, u32[]{:S(2)}, u32[]{:S(2)}) collective-permute-start(bf16[296,768]{1,0:T(8,128)(2,1)} %get-tuple-element.254), channel_id=1, source_target_pairs={{0,16},{16,0},{1,17},{17,1},{2,18},{18,2},{3,19},{19,3},{4,20},{20... | collective-permute-start | bytes 1363976 | tf_op jit(solution)/shard_map/ppermute | solution.py:561
  230.5 24.4 %collective-permute-start.43 = (bf16[296,768]{1,0:T(8,128)(2,1)S(1)}, bf16[296,768]{1,0:T(8,128)(2,1)}, u32[]{:S(2)}, u32[]{:S(2)}) collective-permute-start(bf16[296,768]{1,0:T(8,128)(2,1)S(1)} %get-tuple-element.255), channel_id=1, source_target_pairs={{0,24},{8,16},{16,8},{24,0},{1,25},{9,17},{17,9},{25,1},{2,26},{10... | collective-permute-start | bytes 1363976 | tf_op jit(solution)/shard_map/ppermute | solution.py:584
  232.0 22.0 %collective-permute-start.44 = (bf16[216,768]{1,0:T(8,128)(2,1)}, bf16[216,768]{1,0:T(8,128)(2,1)}, u32[]{:S(2)}, u32[]{:S(2)}) collective-permute-start(bf16[216,768]{1,0:T(8,128)(2,1)} %get-tuple-element.257), channel_id=1, source_target_pairs={{0,1},{1,2},{2,3},{3,0},{4,5},{5,6},{6,7},{7,4},{8,9},{9,10},{10,1... | collective-permute-start | bytes 995336 | tf_op jit(solution)/shard_map/ppermute | solution.py:542
  232.0 22.1 %collective-permute-start.45 = (bf16[216,768]{1,0:T(8,128)(2,1)}, bf16[216,768]{1,0:T(8,128)(2,1)}, u32[]{:S(2)}, u32[]{:S(2)}) collective-permute-start(bf16[216,768]{1,0:T(8,128)(2,1)} %get-tuple-element.258), channel_id=1, source_target_pairs={{0,2},{1,3},{2,0},{3,1},{4,6},{5,7},{6,4},{7,5},{8,10},{9,11},{10,... | collective-permute-start | bytes 995336 | tf_op jit(solution)/shard_map/ppermute | solution.py:542
  256.6 7.4 %collective-permute-start.48 = (bf16[80,768]{1,0:T(8,128)(2,1)S(1)}, bf16[80,768]{1,0:T(8,128)(2,1)S(1)}, u32[]{:S(2)}, u32[]{:S(2)}) collective-permute-start(bf16[80,768]{1,0:T(8,128)(2,1)S(1)} %get-tuple-element.338), channel_id=1, source_target_pairs={{0,3},{1,0},{2,1},{3,2},{4,7},{5,4},{6,5},{7,6},{8,11},{9,8},{10,9... | collective-permute-start | bytes 368648 | tf_op jit(solution)/shard_map/ppermute | solution.py:542
  257.5 11.6 %collective-permute-start.47 = (bf16[80,768]{1,0:T(8,128)(2,1)S(1)}, bf16[80,768]{1,0:T(8,128)(2,1)S(1)}, u32[]{:S(2)}, u32[]{:S(2)}) collective-permute-start(bf16[80,768]{1,0:T(8,128)(2,1)S(1)} %get-tuple-element.337), channel_id=1, source_target_pairs={{0,2},{1,3},{2,0},{3,1},{4,6},{5,7},{6,4},{7,5},{8,10},{9,11},{10,... | collective-permute-start | bytes 368648 | tf_op jit(solution)/shard_map/ppermute | solution.py:542
  261.8 16.7 %collective-permute-start.46 = (bf16[80,768]{1,0:T(8,128)(2,1)S(1)}, bf16[80,768]{1,0:T(8,128)(2,1)S(1)}, u32[]{:S(2)}, u32[]{:S(2)}) collective-permute-start(bf16[80,768]{1,0:T(8,128)(2,1)S(1)} %get-tuple-element.336), channel_id=1, source_target_pairs={{0,1},{1,2},{2,3},{3,0},{4,5},{5,6},{6,7},{7,4},{8,9},{9,10},{10,1... | collective-permute-start | bytes 368648 | tf_op jit(solution)/shard_map/ppermute | solution.py:542
  261.9 18.8 %collective-permute-start.49 = (bf16[216,768]{1,0:T(8,128)(2,1)S(1)}, bf16[216,768]{1,0:T(8,128)(2,1)S(1)}, u32[]{:S(2)}, u32[]{:S(2)}) collective-permute-start(bf16[216,768]{1,0:T(8,128)(2,1)S(1)} %copy-done.22), channel_id=1, source_target_pairs={{0,3},{1,0},{2,1},{3,2},{4,7},{5,4},{6,5},{7,6},{8,11},{9,8},{10,9... | collective-permute-start | bytes 995336 | tf_op jit(solution)/shard_map/ppermute | solution.py:542
  (35 other events, 173.8 us)
where the time goes:
time: 287 us; the launch traced here: 284 us
  Pallas kernels  111 us (39%)
  waiting for transfers between devices  61.6 us (21%)
  starting transfers between devices  50.4 us (18%)
  other arithmetic  34.3 us (12%)
  local copies, waits for them, and re-layouts  24.8 us (9%)
    pallas_call x5, Pallas kernels, call(): return run(*ins)  111 us
    ppermute x33, waiting for transfers between devices, swapped(): return lax.ppermute(block, axis, self.swap)  46 us
    ppermute x33, starting transfers between devices, swapped(): return lax.ppermute(block, axis, self.swap)  27.1 us
    ppermute x15, starting transfers between devices, turn(): return lax.ppermute(block, 'z', [(i, (i + k) % 4) for i in range(4)])  21.3 us
    ppermute x15, waiting for transfers between devices, turn(): return lax.ppermute(block, 'z', [(i, (i + k) % 4) for i in range(4)])  15.6 us
  transfers between devices with their start and end apart: 50, of which 13 were waited for; matrix products, arithmetic and copies ran while one was open for 15% of the time, Pallas kernels for 39%

commit v1 on v0

--- a/solution.py
+++ b/solution.py
@@ -144,6 +144,10 @@
         copy.wait()
 
 
+def column(masked, seq):
+    return jnp.transpose(masked[seq])[:, :1]
+
+
 def attention_kernel(where_ref, tokens, masked, vector, *rest):
     pieces, rest = rest[:8], rest[8:]
     qkv, softs, context, normed_one, params, weights, sems = rest
@@ -154,7 +158,7 @@
         columns = weights[:, 4 * D : 4 * D + 128].astype(F32)
         params[...] = jnp.transpose(columns)[:8]
 
-    start = jnp.where(masked[...] == 1.0, vector[...], tokens[...].astype(F32))
+    start = jnp.where(column(masked, 0) == 1.0, vector[...], tokens[...].astype(F32))
     unit, _ = normalize(start)
     first = (unit * params[0:1] + params[1:2]).astype(BF16)
     normed_one[...] = first
@@ -378,13 +382,14 @@
         wait_all(copies())
 
     grad_one = dot_nt(grad_qkv[here, :], weights[...])
-    start = jnp.where(masked[...] == 1.0, vector[...], tokens[...].astype(F32))
+    hidden_row = column(masked, 0) == 1.0
+    start = jnp.where(hidden_row, vector[...], tokens[...].astype(F32))
     unit, inverse = normalize(start)
     grad_start = normalize_back(grad_one, unit, inverse, params[0:1])
     sums[3:4] += total(grad_one * unit)
     sums[4:5] += total(grad_one)
-    sums[2:3] += total(jnp.where(masked[...] == 1.0, grad_start, 0.0))
-    kept = jnp.where(masked[...] == 1.0, 0.0, grad_start)
+    sums[2:3] += total(jnp.where(hidden_row, grad_start, 0.0))
+    kept = jnp.where(hidden_row, 0.0, grad_start)
     for seq in range(normed_one.shape[0] // SEQ):
         pl.when(step == seq)(functools.partial(put_rows, grad_tokens, kept, seq))
 
@@ -440,7 +445,7 @@
         wait_all(copies)
         for seq in range(tokens.shape[0] // SEQ):
             at = pl.ds(seq * SEQ, SEQ)
-            start = jnp.where(masked[at, :] == 1.0, vector[...], tokens[at, :].astype(F32))
+            start = jnp.where(column(masked, seq) == 1.0, vector[...], tokens[at, :].astype(F32))
             hidden = start + dot(context[at, :], w_out[...])
             out[at, :] = hidden
             unit, _ = normalize(hidden)
@@ -798,17 +803,18 @@
             modality.reshape(seqs, LEN)[:, 0],
         ]
     )
-    tokens = lay(tokens, seqs)
-    ring, where_ref, tokens = tie(ring, where_ref, tokens)
+    masked = jnp.broadcast_to(masked.reshape(seqs, 1, SEQ), (seqs, 8, SEQ)).astype(F32)
+    ring, where_ref = tie(ring, where_ref)
 
     own = net.ring(ring, part)
     near = net.square(own)
     text, _ = tie(pack_expert(w_up[1], w_down[1]), own)
     ring_text = net.turns(text)
-    masked = masked.astype(F32).reshape(rows, 1)
+    tokens, cotangent, _ = tie(tokens, cotangent, own)
+    tokens = lay(tokens, seqs)
     cotangent = lay(cotangent, seqs)
     vector = mask_vector.astype(F32).reshape(1, D)
-    near, masked, place, cotangent, vector = tie(near, masked, place, cotangent, vector)
+    near, place, tokens, cotangent, vector = tie(near, place, tokens, cotangent, vector)
     pieces = net.square_cores(near)
     own_text = net.ring(ring_text, part)
     pieces, own_text, image = tie(pieces, own_text, pack_expert(w_up[0], w_down[0]))
@@ -819,7 +825,7 @@
         attention_kernel,
         seqs,
         (where_ref, tokens, masked, vector, *pieces),
-        [by_step((SEQ, D)), by_step((SEQ, 1)), whole((1, D))] + [ANY] * 8,
+        [by_step((SEQ, D)), by_step((1, 8, SEQ)), whole((1, D))] + [ANY] * 8,
         [
             ((rows, 3 * D), BF16),
             ((seqs, H // 2, SEQ, 2 * SEQ), F32),
@@ -844,7 +850,6 @@
     near_text = net.corner(near_text)
     last, image = tie(net.last(near_text), net.ring(image, part))
     pieces_text = net.cores_of(near_text, last)
-    image, pieces_text = tie(image, pieces_text)
     near_image = net.sides(image)
 
     block = (ROWS_ONE, D)
@@ -889,7 +894,7 @@
         feed_text_kernel,
         4,
         (where_ref, tokens, masked, vector, context, params, *pieces_text, *pieces),
-        [whole((rows, D)), whole((rows, 1)), whole((1, D)), whole((rows, D)), whole((8, D))]
+        [whole((rows, D)), whole((seqs, 8, SEQ)), whole((1, D)), whole((rows, D)), whole((8, D))]
         + [ANY] * 18,
         [((rows, D), F32), ((rows, D), BF16)],
         [whole((rows, D))] * 2,
@@ -920,7 +925,7 @@
             by_step((SEQ, D)),
             whole((rows, D)),
             by_step((SEQ, D)),
-            by_step((SEQ, 1)),
+            by_step((1, 8, SEQ)),
             whole((1, D)),
             whole((8, D)),
             whole((8, D)),

time: 287 us -> 275 us (0.958)
  waiting for transfers between devices: 61.6 us -> 54.9 us
  other arithmetic: 34.3 us -> 28 us
  starting transfers between devices: 50.4 us -> 47.2 us
    ppermute x33, waiting for transfers between devices: 46 us -> 32.5 us  [swapped(): return lax.ppermute(block, axis, self.swap)]
    ppermute x15, waiting for transfers between devices: 15.6 us -> 22.3 us  [turn(): return lax.ppermute(block, 'z', [(i, (i + k) % 4) for i in range(4)])]
    ppermute x33, starting transfers between devices: 27.1 us -> 22.5 us  [swapped(): return lax.ppermute(block, axis, self.swap)]
    concatenate x2 -> x1, other arithmetic: 5.09 us -> 1.87 us  [lay(): jnp.concatenate([jnp.pad(rows[:, :PATCHES], ((0, 0), (0, HEAD - PATCHES),...]
  transfers between devices with their start and end apart: 50 -> 50, of which waited for: 13 -> 14; matrix products, arithmetic and copies ran while one was open for 15% -> 14% of each run, Pallas kernels for 39% -> 41%
where the time goes in v1:
time: 275 us; the launch traced here: 270 us
  Pallas kernels  112 us (41%)
  waiting for transfers between devices  54.9 us (20%)
  starting transfers between devices  47.2 us (17%)
  other arithmetic  28 us (10%)
  local copies, waits for them, and re-layouts  25.9 us (9%)
    pallas_call x5, Pallas kernels, call(): return run(*ins)  112 us
    ppermute x33, waiting for transfers between devices, swapped(): return lax.ppermute(block, axis, self.swap)  32.5 us
    ppermute x15, starting transfers between devices, turn(): return lax.ppermute(block, 'z', [(i, (i + k) % 4) for i in range(4)])  22.8 us
    ppermute x33, starting transfers between devices, swapped(): return lax.ppermute(block, axis, self.swap)  22.5 us
    ppermute x15, waiting for transfers between devices, turn(): return lax.ppermute(block, 'z', [(i, (i + k) % 4) for i in range(4)])  22.3 us
    reshape x2, local copies, waits for them, and re-layouts, lay(): rows = rows.reshape(seqs, LEN, -1)  5.73 us
  transfers between devices with their start and end apart: 50, of which 14 were waited for; matrix products, arithmetic and copies ran while one was open for 14% of the time, Pallas kernels for 41%

profile of v1, /device:TPU:16, one launch (start us, length us, event | category | flops | bytes accessed | tf_op | source)
XLA Modules:
  0.0 269.9 jit_solution(13807009569150690203)
XLA Ops:
  2.4 1.6 collective-permute-start
  4.4 1.2 collective-permute-start.2
  11.3 4.6 %collective-permute-done = bf16[24,3200]{1,0:T(8,128)(2,1)S(1)} collective-permute-done((bf16[24,3200]{1,0:T(8,128)(2,1)S(1)}, bf16[24,3200]{1,0:T(8,128)(2,1)S(1)}, u32[]{:S(2)}, u32[]{:S(2)}) %collective-permute-start) | collective-permute-done | bytes 153632 | tf_op jit(solution)/shard_map/ppermute | solution.py:547
  17.1 1.6 collective-permute-start.3
  19.0 1.6 collective-permute-start.4
  21.7 2.6 collective-permute-start.10
  24.3 1.3 collective-permute-start.11
  25.6 2.9 %reshape.298 = bf16[4,237,768]{2,1,0:T(8,128)(2,1)} reshape(bf16[948,768]{1,0:T(8,128)(2,1)} %param.13) | data formatting | bytes 2912256 | tf_op jit(solution)/shard_map/reshape | solution.py:511
  28.5 2.9 %reshape.300 = bf16[4,237,768]{2,1,0:T(8,128)(2,1)} reshape(bf16[948,768]{1,0:T(8,128)(2,1)} %param.16) | data formatting | bytes 2912256 | tf_op jit(solution)/shard_map/reshape | solution.py:511
  31.3 2.5 collective-permute-done.3.rest_1_.rest_11_
  33.9 2.5 collective-permute-start.12
  36.3 1.9 slice_select_fusion
  40.4 1.9 fusion.5
  42.2 5.5 %collective-permute-done.4.rest_2_.rest_12_ = bf16[96,3200]{1,0:T(8,128)(2,1)S(1)} collective-permute-done((bf16[96,3200]{1,0:T(8,128)(2,1)S(1)}, bf16[96,3200]{1,0:T(8,128)(2,1)S(1)}, u32[]{:S(2)}, u32[]{:S(2)}) %collective-permute-start.4) | collective-permute-done | bytes 614432 | tf_op jit(solution)/shard_map/ppermute | solution.py:566
  50.3 1.2 collective-permute-done.7.rest_5_.rest_15_
  53.4 1.4 collective-permute-start.14
  54.8 1.8 collective-permute-start.15
  56.6 2.2 collective-permute-start.16
  59.9 23.3 %attention.1 = (bf16[1024,2304]{1,0:T(8,128)(2,1)}, f32[4,6,256,512]{3,2,1,0:T(8,128)}, bf16[1024,768]{1,0:T(8,128)(2,1)}, bf16[1024,768]{1,0:T(8,128)(2,1)}, f32[8,768]{1,0:T(8,128)}) custom-call(s32[15]{0:T(128)} %concatenate.53.where_ref, bf16[1024,768]{1,0:T(8,128)(2,1)} %bitcast.145, f32[4,8,256]{2,1,0:T(8,128)} %broadcast_in_dim.4.masked, ...), custom_call_target="tpu_custom_call" | custom-call | flops 1 | bytes 1 | tf_op jit(solution)/shard_map/attention/pallas_call | solution.py:507
  84.6 1.2 collective-permute-start.19
  85.8 1.3 select_bitcast_fusion.3
  88.5 10.8 %collective-permute-done.18.rest_3_ = bf16[384,768]{1,0:T(8,128)(2,1)S(1)} collective-permute-done((bf16[384,768]{1,0:T(8,128)(2,1)S(1)}, bf16[384,768]{1,0:T(8,128)(2,1)S(1)}, u32[]{:S(2)}, u32[]{:S(2)}) %collective-permute-start.18) | collective-permute-done | bytes 589856 | tf_op jit(solution)/shard_map/ppermute | solution.py:566
  100.8 1.5 collective-permute-start.21
  106.1 21.8 %feed_back.1 = (bf16[4,864,768]{2,1,0:T(8,128)(2,1)}, bf16[3,864,768]{2,1,0:T(8,128)(2,1)}, bf16[864,768]{1,0:T(8,128)(2,1)}, bf16[1024,768]{1,0:T(8,128)(2,1)}, f32[8,768]{1,0:T(8,128)}) custom-call(s32[15]{0:T(128)} %concatenate.53.where_ref, s32[1,1024]{1,0:T(1,128)} %get-tuple-element.175.place, f32[1,768]{1,0:T(1,128)} %reshape.341.vector, ...), custom_call_target="tpu_custom_call" | custom-call | flops 1 | bytes 1 | tf_op jit(solution)/shard_map/feed_back/pallas_call | solution.py:507
  128.5 1.9 slice.218
  130.4 1.9 slice.219
  132.3 2.7 fusion.7
  135.8 1.2 collective-permute-start.29
  137.8 1.3 collective-permute-start.32
  139.1 17.2 %feed_text.1 = (f32[1024,768]{1,0:T(8,128)}, bf16[1024,768]{1,0:T(8,128)(2,1)}) custom-call(s32[15]{0:T(128)} %concatenate.53.where_ref, bf16[1024,768]{1,0:T(8,128)(2,1)} %bitcast.146, f32[4,8,256]{2,1,0:T(8,128)} %broadcast_in_dim.4.masked, f32[1,768]{1,0:T(1,128)} %reshape.341.vector, bf16[1024,768]{1,0:T(8,128)(2,1)} %get-tuple-element.198.context, ...), custom_call_target="tpu_custom_call" | custom-call | flops 1 | bytes 1 | tf_op jit(solution)/shard_map/feed_text/pallas_call | solution.py:507
  156.3 9.5 %collective-permute-done.31.rest_3_ = bf16[384,768]{1,0:T(8,128)(2,1)} collective-permute-done((bf16[384,768]{1,0:T(8,128)(2,1)}, bf16[384,768]{1,0:T(8,128)(2,1)}, u32[]{:S(2)}, u32[]{:S(2)}) %collective-permute-start.31) | collective-permute-done | bytes 589856 | tf_op jit(solution)/shard_map/ppermute | solution.py:566
  166.4 5.2 %fusion.3 = (bf16[864,768]{1,0:T(8,128)(2,1)}, bf16[864,768]{1,0:T(8,128)(2,1)}) fusion(bf16[432,768]{1,0:T(8,128)(2,1)} %collective-permute-done.28, bf16[3,864,768]{2,1,0:T(8,128)(2,1)S(1)} %collective-permute-done.30, bf16[4,864,768]{2,1,0:T(8,128)(2,1)} %get-tuple-element.221, bf16[432,768]{1,0:T(8,128)(2,1)} %collective-permute-done.29), kind=kLoop, calls=%fused_computation.6 | loop fusion | flops 7962624 | bytes 9289728 | tf_op jit(solution)/shard_map/convert_element_type | solution.py:610
  172.4 1.3 collective-permute-start.35
  174.9 30.4 %attention_back.1 = (bf16[4,304,768]{2,1,0:T(8,128)(2,1)}, bf16[4,304,768]{2,1,0:T(8,128)(2,1)}, f32[948,768]{1,0:T(8,128)}) custom-call(s32[15]{0:T(128)} %concatenate.53.where_ref, bf16[1024,2304]{1,0:T(8,128)(2,1)} %get-tuple-element.166.qkv, f32[4,6,256,512]{3,2,1,0:T(8,128)} %get-tuple-element.167.softs, ...), custom_call_target="tpu_custom_call" | custom-call | flops 1 | bytes 1 | tf_op jit(solution)/shard_map/attention_back/pallas_call | solution.py:507
  206.0 2.4 fusion.18
  211.2 1.3 copy-done.19
  212.5 1.3 fusion.13
  214.5 1.3 collective-permute-start.42
  215.8 1.5 collective-permute-start.43
  217.2 2.0 collective-permute-start.44
  220.0 18.8 %feed_image.1 = bf16[948,768]{1,0:T(8,128)(2,1)} custom-call(s32[15]{0:T(128)} %concatenate.53.where_ref, bf16[1024,768]{1,0:T(8,128)(2,1)} %get-tuple-element.240.rows_in, f32[1024,768]{1,0:T(8,128)} %get-tuple-element.241.before, bf16[768,768]{1,0:T(8,128)(2,1)} %pad_maximum_fusion.3.rest_0_, bf16[768,768]{1,0:T(8,128)(2,1)} %collective-permute-done.20.rest_1_, ...), custom_call_target="tpu_custom_call" | custom-call | flops 1 | bytes 1 | tf_op jit(solution)/shard_map/feed_image/pallas_call | solution.py:507
  238.8 1.8 collective-permute-done.45
  241.4 1.6 fusion.16
  243.2 3.9 %collective-permute-start.47 = (bf16[80,768]{1,0:T(8,128)(2,1)S(1)}, bf16[80,768]{1,0:T(8,128)(2,1)S(1)}, u32[]{:S(2)}, u32[]{:S(2)}) collective-permute-start(bf16[80,768]{1,0:T(8,128)(2,1)S(1)} %get-tuple-element.317), channel_id=1, source_target_pairs={{0,2},{1,3},{2,0},{3,1},{4,6},{5,7},{6,4},{7,5},{8,10},{9,11},{10,... | collective-permute-start | bytes 368648 | tf_op jit(solution)/shard_map/ppermute | solution.py:547
  247.0 1.8 collective-permute-start.46
  249.2 5.8 %collective-permute-done.47 = bf16[80,768]{1,0:T(8,128)(2,1)S(1)} collective-permute-done((bf16[80,768]{1,0:T(8,128)(2,1)S(1)}, bf16[80,768]{1,0:T(8,128)(2,1)S(1)}, u32[]{:S(2)}, u32[]{:S(2)}) %collective-permute-start.47) | collective-permute-done | bytes 122912 | tf_op jit(solution)/shard_map/ppermute | solution.py:547
  255.0 9.2 %collective-permute-done.46 = bf16[80,768]{1,0:T(8,128)(2,1)S(1)} collective-permute-done((bf16[80,768]{1,0:T(8,128)(2,1)S(1)}, bf16[80,768]{1,0:T(8,128)(2,1)S(1)}, u32[]{:S(2)}, u32[]{:S(2)}) %collective-permute-start.46) | collective-permute-done | bytes 122912 | tf_op jit(solution)/shard_map/ppermute | solution.py:547
  266.3 1.2 add_add_fusion
  (204 shorter events, 40.2 us)
Async XLA Ops:
  2.4 13.5 %collective-permute-start = (bf16[24,3200]{1,0:T(8,128)(2,1)S(1)}, bf16[24,3200]{1,0:T(8,128)(2,1)S(1)}, u32[]{:S(2)}, u32[]{:S(2)}) collective-permute-start(bf16[24,3200]{1,0:T(8,128)(2,1)S(1)} %fusion.15), channel_id=1, source_target_pairs={{0,1},{1,2},{2,3},{3,0},{4,5},{5,6},{6,7},{7,4},{8,9},{9,10},{10,1... | collective-permute-start | bytes 460808 | tf_op jit(solution)/shard_map/ppermute | solution.py:547
  4.0 11.9 %collective-permute-start.1 = (bf16[24,3200]{1,0:T(8,128)(2,1)S(1)}, bf16[24,3200]{1,0:T(8,128)(2,1)S(1)}, u32[]{:S(2)}, u32[]{:S(2)}) collective-permute-start(bf16[24,3200]{1,0:T(8,128)(2,1)S(1)} %fusion.15), channel_id=1, source_target_pairs={{0,2},{1,3},{2,0},{3,1},{4,6},{5,7},{6,4},{7,5},{8,10},{9,11},{10,... | collective-permute-start | bytes 460808 | tf_op jit(solution)/shard_map/ppermute | solution.py:547
  4.4 12.5 %collective-permute-start.2 = (bf16[24,3200]{1,0:T(8,128)(2,1)S(1)}, bf16[24,3200]{1,0:T(8,128)(2,1)S(1)}, u32[]{:S(2)}, u32[]{:S(2)}) collective-permute-start(bf16[24,3200]{1,0:T(8,128)(2,1)S(1)} %fusion.15), channel_id=1, source_target_pairs={{0,3},{1,0},{2,1},{3,2},{4,7},{5,4},{6,5},{7,6},{8,11},{9,8},{10,9... | collective-permute-start | bytes 460808 | tf_op jit(solution)/shard_map/ppermute | solution.py:547
  17.1 16.8 %collective-permute-start.3 = (bf16[96,3200]{1,0:T(8,128)(2,1)S(1)}, bf16[96,3200]{1,0:T(8,128)(2,1)S(1)}, u32[]{:S(2)}, u32[]{:S(2)}) collective-permute-start(bf16[96,3200]{1,0:T(8,128)(2,1)S(1)} %bitcast.148), channel_id=1, source_target_pairs={{0,8},{8,0},{1,9},{9,1},{2,10},{10,2},{3,11},{11,3},{4,12},{12,4},... | collective-permute-start | bytes 1843208 | tf_op jit(solution)/shard_map/ppermute | solution.py:566
  19.0 28.7 %collective-permute-start.4 = (bf16[96,3200]{1,0:T(8,128)(2,1)S(1)}, bf16[96,3200]{1,0:T(8,128)(2,1)S(1)}, u32[]{:S(2)}, u32[]{:S(2)}) collective-permute-start(bf16[96,3200]{1,0:T(8,128)(2,1)S(1)} %bitcast.149), channel_id=1, source_target_pairs={{0,16},{16,0},{1,17},{17,1},{2,18},{18,2},{3,19},{19,3},{4,20},{20... | collective-permute-start | bytes 1843208 | tf_op jit(solution)/shard_map/ppermute | solution.py:566
  20.6 27.1 %collective-permute-start.5 = (bf16[96,3200]{1,0:T(8,128)(2,1)S(1)}, bf16[96,3200]{1,0:T(8,128)(2,1)}, u32[]{:S(2)}, u32[]{:S(2)}) collective-permute-start(bf16[96,3200]{1,0:T(8,128)(2,1)S(1)} %bitcast.150), channel_id=1, source_target_pairs={{0,24},{8,16},{16,8},{24,0},{1,25},{9,17},{17,9},{25,1},{2,26},{10... | collective-permute-start | bytes 1843208 | tf_op jit(solution)/shard_map/ppermute | solution.py:589
  21.7 26.6 %collective-permute-start.10 = (bf16[192,768]{1,0:T(8,128)(2,1)S(1)}, bf16[192,768]{1,0:T(8,128)(2,1)S(1)}, u32[]{:S(2)}, u32[]{:S(2)}) collective-permute-start(bf16[192,768]{1,0:T(8,128)(2,1)S(1)} %pad_maximum_fusion.9), channel_id=1, source_target_pairs={{0,1},{1,2},{2,3},{3,0},{4,5},{5,6},{6,7},{7,4},{8,9},{9,10},{10,1... | collective-permute-start | bytes 884744 | tf_op jit(solution)/shard_map/ppermute | solution.py:547
  24.3 24.1 %collective-permute-start.11 = (bf16[192,768]{1,0:T(8,128)(2,1)S(1)}, bf16[192,768]{1,0:T(8,128)(2,1)}, u32[]{:S(2)}, u32[]{:S(2)}) collective-permute-start(bf16[192,768]{1,0:T(8,128)(2,1)S(1)} %pad_maximum_fusion.9), channel_id=1, source_target_pairs={{0,2},{1,3},{2,0},{3,1},{4,6},{5,7},{6,4},{7,5},{8,10},{9,11},{10,... | collective-permute-start | bytes 884744 | tf_op jit(solution)/shard_map/ppermute | solution.py:547
  33.9 15.0 %collective-permute-start.12 = (bf16[192,768]{1,0:T(8,128)(2,1)S(1)}, bf16[192,768]{1,0:T(8,128)(2,1)S(1)}, u32[]{:S(2)}, u32[]{:S(2)}) collective-permute-start(bf16[192,768]{1,0:T(8,128)(2,1)S(1)} %pad_maximum_fusion.9), channel_id=1, source_target_pairs={{0,3},{1,0},{2,1},{3,2},{4,7},{5,4},{6,5},{7,6},{8,11},{9,8},{10,9... | collective-permute-start | bytes 884744 | tf_op jit(solution)/shard_map/ppermute | solution.py:547
  47.8 3.8 %collective-permute-start.7 = (bf16[96,3200]{1,0:T(8,128)(2,1)S(1)}, bf16[96,3200]{1,0:T(8,128)(2,1)S(1)}, u32[]{:S(2)}, u32[]{:S(2)}) collective-permute-start(bf16[96,3200]{1,0:T(8,128)(2,1)S(1)} %collective-permute-done.3.rest_1_.rest_11_), channel_id=1, source_target_pairs={{0,4},{4,0},{1,5},{5,1},{2,6},{6,2},{3,7},{7,3},{8,12},{12,8},{9,1... | collective-permute-start | bytes 1843208 | tf_op jit(solution)/shard_map/ppermute | solution.py:566
  48.3 4.2 %collective-permute-start.8 = (bf16[96,3200]{1,0:T(8,128)(2,1)S(1)}, bf16[96,3200]{1,0:T(8,128)(2,1)S(1)}, u32[]{:S(2)}, u32[]{:S(2)}) collective-permute-start(bf16[96,3200]{1,0:T(8,128)(2,1)S(1)} %collective-permute-done.4.rest_2_.rest_12_), channel_id=1, source_target_pairs={{0,4},{4,0},{1,5},{5,1},{2,6},{6,2},{3,7},{7,3},{8,12},{12,8},{9,1... | collective-permute-start | bytes 1843208 | tf_op jit(solution)/shard_map/ppermute | solution.py:566
  48.4 4.1 %collective-permute-start.9 = (bf16[96,3200]{1,0:T(8,128)(2,1)}, bf16[96,3200]{1,0:T(8,128)(2,1)S(1)}, u32[]{:S(2)}, u32[]{:S(2)}) collective-permute-start(bf16[96,3200]{1,0:T(8,128)(2,1)} %collective-permute-done.5.rest_3_.rest_13_), channel_id=1, source_target_pairs={{0,4},{4,0},{1,5},{5,1},{2,6},{6,2},{3,7},{7,3},{8,12},{12,8},{9,1... | collective-permute-start | bytes 1843208 | tf_op jit(solution)/shard_map/ppermute | solution.py:566
  52.5 30.8 %collective-permute-start.13 = (bf16[768,768]{1,0:T(8,128)(2,1)S(1)}, bf16[768,768]{1,0:T(8,128)(2,1)S(1)}, u32[]{:S(2)}, u32[]{:S(2)}) collective-permute-start(bf16[768,768]{1,0:T(8,128)(2,1)S(1)} %pad_maximum_fusion.1.rest_0_), channel_id=1, source_target_pairs={{0,8},{8,0},{1,9},{9,1},{2,10},{10,2},{3,11},{11,3},{4,12},{12,4},... | collective-permute-start | bytes 3538952 | tf_op jit(solution)/shard_map/ppermute | solution.py:566
  53.4 29.9 %collective-permute-start.14 = (bf16[768,768]{1,0:T(8,128)(2,1)S(1)}, bf16[768,768]{1,0:T(8,128)(2,1)S(1)}, u32[]{:S(2)}, u32[]{:S(2)}) collective-permute-start(bf16[768,768]{1,0:T(8,128)(2,1)S(1)} %pad_maximum_fusion.1.rest_0_), channel_id=1, source_target_pairs={{0,16},{16,0},{1,17},{17,1},{2,18},{18,2},{3,19},{19,3},{4,20},{20... | collective-permute-start | bytes 3538952 | tf_op jit(solution)/shard_map/ppermute | solution.py:566
  54.8 28.4 %collective-permute-start.15 = (bf16[192,768]{1,0:T(8,128)(2,1)S(1)}, bf16[192,768]{1,0:T(8,128)(2,1)}, u32[]{:S(2)}, u32[]{:S(2)}) collective-permute-start(bf16[192,768]{1,0:T(8,128)(2,1)S(1)} %pad_maximum_fusion.10), channel_id=1, source_target_pairs={{0,1},{1,2},{2,3},{3,0},{4,5},{5,6},{6,7},{7,4},{8,9},{9,10},{10,1... | collective-permute-start | bytes 884744 | tf_op jit(solution)/shard_map/ppermute | solution.py:547
  56.6 26.7 %collective-permute-start.16 = (bf16[192,768]{1,0:T(8,128)(2,1)S(1)}, bf16[192,768]{1,0:T(8,128)(2,1)}, u32[]{:S(2)}, u32[]{:S(2)}) collective-permute-start(bf16[192,768]{1,0:T(8,128)(2,1)S(1)} %pad_maximum_fusion.10), channel_id=1, source_target_pairs={{0,2},{1,3},{2,0},{3,1},{4,6},{5,7},{6,4},{7,5},{8,10},{9,11},{10,... | collective-permute-start | bytes 884744 | tf_op jit(solution)/shard_map/ppermute | solution.py:547
  58.8 24.5 %collective-permute-start.17 = (bf16[192,768]{1,0:T(8,128)(2,1)S(1)}, bf16[192,768]{1,0:T(8,128)(2,1)}, u32[]{:S(2)}, u32[]{:S(2)}) collective-permute-start(bf16[192,768]{1,0:T(8,128)(2,1)S(1)} %pad_maximum_fusion.10), channel_id=1, source_target_pairs={{0,3},{1,0},{2,1},{3,2},{4,7},{5,4},{6,5},{7,6},{8,11},{9,8},{10,9... | collective-permute-start | bytes 884744 | tf_op jit(solution)/shard_map/ppermute | solution.py:547
  83.3 19.0 %collective-permute-start.23 = (bf16[768,768]{1,0:T(8,128)(2,1)S(1)}, bf16[768,768]{1,0:T(8,128)(2,1)S(1)}, u32[]{:S(2)}, u32[]{:S(2)}) collective-permute-start(bf16[768,768]{1,0:T(8,128)(2,1)S(1)} %collective-permute-done.13.rest_1_), channel_id=1, source_target_pairs={{0,4},{4,0},{1,5},{5,1},{2,6},{6,2},{3,7},{7,3},{8,12},{12,8},{9,1... | collective-permute-start | bytes 3538952 | tf_op jit(solution)/shard_map/ppermute | solution.py:566
  83.5 19.4 %collective-permute-start.24 = (bf16[768,768]{1,0:T(8,128)(2,1)S(1)}, bf16[768,768]{1,0:T(8,128)(2,1)S(1)}, u32[]{:S(2)}, u32[]{:S(2)}) collective-permute-start(bf16[768,768]{1,0:T(8,128)(2,1)S(1)} %collective-permute-done.14.rest_2_), channel_id=1, source_target_pairs={{0,4},{4,0},{1,5},{5,1},{2,6},{6,2},{3,7},{7,3},{8,12},{12,8},{9,1... | collective-permute-start | bytes 3538952 | tf_op jit(solution)/shard_map/ppermute | solution.py:566
  84.0 15.3 %collective-permute-start.18 = (bf16[384,768]{1,0:T(8,128)(2,1)S(1)}, bf16[384,768]{1,0:T(8,128)(2,1)S(1)}, u32[]{:S(2)}, u32[]{:S(2)}) collective-permute-start(bf16[384,768]{1,0:T(8,128)(2,1)S(1)} %slice.210), channel_id=1, source_target_pairs={{0,16},{16,0},{1,17},{17,1},{2,18},{18,2},{3,19},{19,3},{4,20},{20... | collective-permute-start | bytes 1769480 | tf_op jit(solution)/shard_map/ppermute | solution.py:566
  84.6 15.0 %collective-permute-start.19 = (bf16[384,768]{1,0:T(8,128)(2,1)S(1)}, bf16[384,768]{1,0:T(8,128)(2,1)S(1)}, u32[]{:S(2)}, u32[]{:S(2)}) collective-permute-start(bf16[384,768]{1,0:T(8,128)(2,1)S(1)} %slice.211), channel_id=1, source_target_pairs={{0,8},{8,0},{1,9},{9,1},{2,10},{10,2},{3,11},{11,3},{4,12},{12,4},... | collective-permute-start | bytes 1769480 | tf_op jit(solution)/shard_map/ppermute | solution.py:566
  85.8 16.6 %collective-permute-start.22 = (bf16[768,768]{1,0:T(8,128)(2,1)S(1)}, bf16[768,768]{1,0:T(8,128)(2,1)S(1)}, u32[]{:S(2)}, u32[]{:S(2)}) collective-permute-start(bf16[768,768]{1,0:T(8,128)(2,1)S(1)} %pad_maximum_fusion.1.rest_0_), channel_id=1, source_target_pairs={{0,4},{4,0},{1,5},{5,1},{2,6},{6,2},{3,7},{7,3},{8,12},{12,8},{9,1... | collective-permute-start | bytes 3538952 | tf_op jit(solution)/shard_map/ppermute | solution.py:566
  99.7 28.2 %collective-permute-start.20 = (bf16[768,768]{1,0:T(8,128)(2,1)}, bf16[768,768]{1,0:T(8,128)(2,1)}, u32[]{:S(2)}, u32[]{:S(2)}) collective-permute-start(bf16[768,768]{1,0:T(8,128)(2,1)} %pad_maximum_fusion.3.rest_0_), channel_id=1, source_target_pairs={{0,8},{8,0},{1,9},{9,1},{2,10},{10,2},{3,11},{11,3},{4,12},{12,4},... | collective-permute-start | bytes 3538952 | tf_op jit(solution)/shard_map/ppermute | solution.py:566
  100.8 27.1 %collective-permute-start.21 = (bf16[768,768]{1,0:T(8,128)(2,1)}, bf16[768,768]{1,0:T(8,128)(2,1)}, u32[]{:S(2)}, u32[]{:S(2)}) collective-permute-start(bf16[768,768]{1,0:T(8,128)(2,1)} %pad_maximum_fusion.3.rest_0_), channel_id=1, source_target_pairs={{0,16},{16,0},{1,17},{17,1},{2,18},{18,2},{3,19},{19,3},{4,20},{20... | collective-permute-start | bytes 3538952 | tf_op jit(solution)/shard_map/ppermute | solution.py:566
  102.4 2.8 %collective-permute-start.26 = (bf16[384,768]{1,0:T(8,128)(2,1)S(1)}, bf16[384,768]{1,0:T(8,128)(2,1)S(1)}, u32[]{:S(2)}, u32[]{:S(2)}) collective-permute-start(bf16[384,768]{1,0:T(8,128)(2,1)S(1)} %collective-permute-done.19.rest_4_), channel_id=1, source_target_pairs={{0,4},{4,0},{1,5},{5,1},{2,6},{6,2},{3,7},{7,3},{8,12},{12,8},{9,1... | collective-permute-start | bytes 1769480 | tf_op jit(solution)/shard_map/ppermute | solution.py:566
  127.9 4.4 %collective-permute-start.27 = (bf16[864,768]{1,0:T(8,128)(2,1)}, bf16[864,768]{1,0:T(8,128)(2,1)S(1)}, u32[]{:S(2)}, u32[]{:S(2)}) collective-permute-start(bf16[864,768]{1,0:T(8,128)(2,1)} %get-tuple-element.188), channel_id=1, source_target_pairs={{0,4},{4,0},{1,5},{5,1},{2,6},{6,2},{3,7},{7,3},{8,12},{12,8},{9,1... | collective-permute-start | bytes 3981320 | tf_op jit(solution)/shard_map/ppermute | solution.py:566
  135.0 30.8 %collective-permute-start.30 = (bf16[3,864,768]{2,1,0:T(8,128)(2,1)}, bf16[3,864,768]{2,1,0:T(8,128)(2,1)S(1)}, u32[]{:S(2)}, u32[]{:S(2)}) collective-permute-start(bf16[3,864,768]{2,1,0:T(8,128)(2,1)} %get-tuple-element.194), channel_id=1, source_target_pairs={{0,4},{4,0},{1,5},{5,1},{2,6},{6,2},{3,7},{7,3},{8,12},{12,8},{9,1... | collective-permute-start | bytes 11943944 | tf_op jit(solution)/shard_map/ppermute | solution.py:566
  135.1 30.7 %collective-permute-start.28 = (bf16[432,768]{1,0:T(8,128)(2,1)}, bf16[432,768]{1,0:T(8,128)(2,1)}, u32[]{:S(2)}, u32[]{:S(2)}) collective-permute-start(bf16[432,768]{1,0:T(8,128)(2,1)} %get-tuple-element.192), channel_id=1, source_target_pairs={{0,8},{8,0},{1,9},{9,1},{2,10},{10,2},{3,11},{11,3},{4,12},{12,4},... | collective-permute-start | bytes 1990664 | tf_op jit(solution)/shard_map/ppermute | solution.py:566
  135.8 30.0 %collective-permute-start.29 = (bf16[432,768]{1,0:T(8,128)(2,1)}, bf16[432,768]{1,0:T(8,128)(2,1)}, u32[]{:S(2)}, u32[]{:S(2)}) collective-permute-start(bf16[432,768]{1,0:T(8,128)(2,1)} %get-tuple-element.193), channel_id=1, source_target_pairs={{0,16},{16,0},{1,17},{17,1},{2,18},{18,2},{3,19},{19,3},{4,20},{20... | collective-permute-start | bytes 1990664 | tf_op jit(solution)/shard_map/ppermute | solution.py:566
  137.0 28.8 %collective-permute-start.31 = (bf16[384,768]{1,0:T(8,128)(2,1)}, bf16[384,768]{1,0:T(8,128)(2,1)}, u32[]{:S(2)}, u32[]{:S(2)}) collective-permute-start(bf16[384,768]{1,0:T(8,128)(2,1)} %slice.218), channel_id=1, source_target_pairs={{0,16},{16,0},{1,17},{17,1},{2,18},{18,2},{3,19},{19,3},{4,20},{20... | collective-permute-start | bytes 1769480 | tf_op jit(solution)/shard_map/ppermute | solution.py:566
  137.8 27.9 %collective-permute-start.32 = (bf16[384,768]{1,0:T(8,128)(2,1)}, bf16[384,768]{1,0:T(8,128)(2,1)}, u32[]{:S(2)}, u32[]{:S(2)}) collective-permute-start(bf16[384,768]{1,0:T(8,128)(2,1)} %slice.219), channel_id=1, source_target_pairs={{0,8},{8,0},{1,9},{9,1},{2,10},{10,2},{3,11},{11,3},{4,12},{12,4},... | collective-permute-start | bytes 1769480 | tf_op jit(solution)/shard_map/ppermute | solution.py:566
  165.8 5.8 %collective-permute-start.33 = (bf16[384,768]{1,0:T(8,128)(2,1)}, bf16[384,768]{1,0:T(8,128)(2,1)S(1)}, u32[]{:S(2)}, u32[]{:S(2)}) collective-permute-start(bf16[384,768]{1,0:T(8,128)(2,1)} %collective-permute-done.31.rest_3_), channel_id=1, source_target_pairs={{0,4},{4,0},{1,5},{5,1},{2,6},{6,2},{3,7},{7,3},{8,12},{12,8},{9,1... | collective-permute-start | bytes 1769480 | tf_op jit(solution)/shard_map/ppermute | solution.py:566
  165.9 5.7 %collective-permute-start.34 = (bf16[384,768]{1,0:T(8,128)(2,1)}, bf16[384,768]{1,0:T(8,128)(2,1)S(1)}, u32[]{:S(2)}, u32[]{:S(2)}) collective-permute-start(bf16[384,768]{1,0:T(8,128)(2,1)} %collective-permute-done.32.rest_4_), channel_id=1, source_target_pairs={{0,4},{4,0},{1,5},{5,1},{2,6},{6,2},{3,7},{7,3},{8,12},{12,8},{9,1... | collective-permute-start | bytes 1769480 | tf_op jit(solution)/shard_map/ppermute | solution.py:566
  172.4 33.0 %collective-permute-start.35 = (bf16[864,768]{1,0:T(8,128)(2,1)}, bf16[864,768]{1,0:T(8,128)(2,1)S(1)}, u32[]{:S(2)}, u32[]{:S(2)}) collective-permute-start(bf16[864,768]{1,0:T(8,128)(2,1)} %get-tuple-element.214), channel_id=1, source_target_pairs={{0,8},{8,0},{1,9},{9,1},{2,10},{10,2},{3,11},{11,3},{4,12},{12,4},... | collective-permute-start | bytes 3981320 | tf_op jit(solution)/shard_map/ppermute | solution.py:566
  173.7 31.7 %collective-permute-start.36 = (bf16[864,768]{1,0:T(8,128)(2,1)}, bf16[864,768]{1,0:T(8,128)(2,1)S(1)}, u32[]{:S(2)}, u32[]{:S(2)}) collective-permute-start(bf16[864,768]{1,0:T(8,128)(2,1)} %get-tuple-element.215), channel_id=1, source_target_pairs={{0,16},{16,0},{1,17},{17,1},{2,18},{18,2},{3,19},{19,3},{4,20},{20... | collective-permute-start | bytes 3981320 | tf_op jit(solution)/shard_map/ppermute | solution.py:566
  174.4 30.9 %collective-permute-start.37 = (bf16[768,768]{1,0:T(8,128)(2,1)}, bf16[768,768]{1,0:T(8,128)(2,1)}, u32[]{:S(2)}, u32[]{:S(2)}) collective-permute-start(bf16[768,768]{1,0:T(8,128)(2,1)} %pad_maximum_fusion.3.rest_0_), channel_id=1, source_target_pairs={{0,4},{4,0},{1,5},{5,1},{2,6},{6,2},{3,7},{7,3},{8,12},{12,8},{9,1... | collective-permute-start | bytes 3538952 | tf_op jit(solution)/shard_map/ppermute | solution.py:566
  174.4 31.0 %collective-permute-start.38 = (bf16[768,768]{1,0:T(8,128)(2,1)}, bf16[768,768]{1,0:T(8,128)(2,1)}, u32[]{:S(2)}, u32[]{:S(2)}) collective-permute-start(bf16[768,768]{1,0:T(8,128)(2,1)} %collective-permute-done.20.rest_1_), channel_id=1, source_target_pairs={{0,4},{4,0},{1,5},{5,1},{2,6},{6,2},{3,7},{7,3},{8,12},{12,8},{9,1... | collective-permute-start | bytes 3538952 | tf_op jit(solution)/shard_map/ppermute | solution.py:566
  174.9 30.5 %collective-permute-start.39 = (bf16[768,768]{1,0:T(8,128)(2,1)}, bf16[768,768]{1,0:T(8,128)(2,1)}, u32[]{:S(2)}, u32[]{:S(2)}) collective-permute-start(bf16[768,768]{1,0:T(8,128)(2,1)} %collective-permute-done.21.rest_2_), channel_id=1, source_target_pairs={{0,4},{4,0},{1,5},{5,1},{2,6},{6,2},{3,7},{7,3},{8,12},{12,8},{9,1... | collective-permute-start | bytes 3538952 | tf_op jit(solution)/shard_map/ppermute | solution.py:566
  205.4 5.8 %collective-permute-start.40 = (bf16[4,304,768]{2,1,0:T(8,128)(2,1)}, bf16[4,304,768]{2,1,0:T(8,128)(2,1)S(1)}, u32[]{:S(2)}, u32[]{:S(2)}) collective-permute-start(bf16[4,304,768]{2,1,0:T(8,128)(2,1)} %get-tuple-element.220), channel_id=1, source_target_pairs={{0,4},{4,0},{1,5},{5,1},{2,6},{6,2},{3,7},{7,3},{8,12},{12,8},{9,1... | collective-permute-start | bytes 5603336 | tf_op jit(solution)/shard_map/ppermute | solution.py:566
  213.7 26.9 %collective-permute-start.41 = (bf16[296,768]{1,0:T(8,128)(2,1)}, bf16[296,768]{1,0:T(8,128)(2,1)S(1)}, u32[]{:S(2)}, u32[]{:S(2)}) collective-permute-start(bf16[296,768]{1,0:T(8,128)(2,1)} %get-tuple-element.233), channel_id=1, source_target_pairs={{0,8},{8,0},{1,9},{9,1},{2,10},{10,2},{3,11},{11,3},{4,12},{12,4},... | collective-permute-start | bytes 1363976 | tf_op jit(solution)/shard_map/ppermute | solution.py:566
  214.5 26.1 %collective-permute-start.42 = (bf16[296,768]{1,0:T(8,128)(2,1)}, bf16[296,768]{1,0:T(8,128)(2,1)S(1)}, u32[]{:S(2)}, u32[]{:S(2)}) collective-permute-start(bf16[296,768]{1,0:T(8,128)(2,1)} %get-tuple-element.234), channel_id=1, source_target_pairs={{0,16},{16,0},{1,17},{17,1},{2,18},{18,2},{3,19},{19,3},{4,20},{20... | collective-permute-start | bytes 1363976 | tf_op jit(solution)/shard_map/ppermute | solution.py:566
  215.8 25.6 %collective-permute-start.43 = (bf16[296,768]{1,0:T(8,128)(2,1)S(1)}, bf16[296,768]{1,0:T(8,128)(2,1)}, u32[]{:S(2)}, u32[]{:S(2)}) collective-permute-start(bf16[296,768]{1,0:T(8,128)(2,1)S(1)} %get-tuple-element.235), channel_id=1, source_target_pairs={{0,24},{8,16},{16,8},{24,0},{1,25},{9,17},{17,9},{25,1},{2,26},{10... | collective-permute-start | bytes 1363976 | tf_op jit(solution)/shard_map/ppermute | solution.py:589
  217.2 21.5 %collective-permute-start.44 = (bf16[216,768]{1,0:T(8,128)(2,1)}, bf16[216,768]{1,0:T(8,128)(2,1)}, u32[]{:S(2)}, u32[]{:S(2)}) collective-permute-start(bf16[216,768]{1,0:T(8,128)(2,1)} %pad_maximum_fusion.6), channel_id=1, source_target_pairs={{0,1},{1,2},{2,3},{3,0},{4,5},{5,6},{6,7},{7,4},{8,9},{9,10},{10,1... | collective-permute-start | bytes 995336 | tf_op jit(solution)/shard_map/ppermute | solution.py:547
  219.2 21.4 %collective-permute-start.45 = (bf16[216,768]{1,0:T(8,128)(2,1)}, bf16[216,768]{1,0:T(8,128)(2,1)}, u32[]{:S(2)}, u32[]{:S(2)}) collective-permute-start(bf16[216,768]{1,0:T(8,128)(2,1)} %pad_maximum_fusion.7), channel_id=1, source_target_pairs={{0,2},{1,3},{2,0},{3,1},{4,6},{5,7},{6,4},{7,5},{8,10},{9,11},{10,... | collective-permute-start | bytes 995336 | tf_op jit(solution)/shard_map/ppermute | solution.py:547
  243.1 6.1 %collective-permute-start.48 = (bf16[80,768]{1,0:T(8,128)(2,1)S(1)}, bf16[80,768]{1,0:T(8,128)(2,1)S(1)}, u32[]{:S(2)}, u32[]{:S(2)}) collective-permute-start(bf16[80,768]{1,0:T(8,128)(2,1)S(1)} %get-tuple-element.318), channel_id=1, source_target_pairs={{0,3},{1,0},{2,1},{3,2},{4,7},{5,4},{6,5},{7,6},{8,11},{9,8},{10,9... | collective-permute-start | bytes 368648 | tf_op jit(solution)/shard_map/ppermute | solution.py:547
  243.2 11.8 %collective-permute-start.47 = (bf16[80,768]{1,0:T(8,128)(2,1)S(1)}, bf16[80,768]{1,0:T(8,128)(2,1)S(1)}, u32[]{:S(2)}, u32[]{:S(2)}) collective-permute-start(bf16[80,768]{1,0:T(8,128)(2,1)S(1)} %get-tuple-element.317), channel_id=1, source_target_pairs={{0,2},{1,3},{2,0},{3,1},{4,6},{5,7},{6,4},{7,5},{8,10},{9,11},{10,... | collective-permute-start | bytes 368648 | tf_op jit(solution)/shard_map/ppermute | solution.py:547
  247.0 17.1 %collective-permute-start.46 = (bf16[80,768]{1,0:T(8,128)(2,1)S(1)}, bf16[80,768]{1,0:T(8,128)(2,1)S(1)}, u32[]{:S(2)}, u32[]{:S(2)}) collective-permute-start(bf16[80,768]{1,0:T(8,128)(2,1)S(1)} %get-tuple-element.316), channel_id=1, source_target_pairs={{0,1},{1,2},{2,3},{3,0},{4,5},{5,6},{6,7},{7,4},{8,9},{9,10},{10,1... | collective-permute-start | bytes 368648 | tf_op jit(solution)/shard_map/ppermute | solution.py:547
  248.9 17.4 %collective-permute-start.49 = (bf16[216,768]{1,0:T(8,128)(2,1)S(1)}, bf16[216,768]{1,0:T(8,128)(2,1)S(1)}, u32[]{:S(2)}, u32[]{:S(2)}) collective-permute-start(bf16[216,768]{1,0:T(8,128)(2,1)S(1)} %copy-done.23), channel_id=1, source_target_pairs={{0,3},{1,0},{2,1},{3,2},{4,7},{5,4},{6,5},{7,6},{8,11},{9,8},{10,9... | collective-permute-start | bytes 995336 | tf_op jit(solution)/shard_map/ppermute | solution.py:547
  (30 other events, 163.0 us)

commit v2 on v1

--- a/solution.py
+++ b/solution.py
@@ -118,25 +118,34 @@
     )
 
 
-def load_expert(where_ref, pieces, up, down, sems):
-    copies = []
+def expert_copies(where_ref, pieces, up, down, sems):
+    ups, downs = [[], [], [], []], []
     for piece, block, first, size in spans(where_ref, pieces, 768):
         if first == 0:
             for chunk in range(4):
-                copies.append(
-                    (
-                        piece.at[pl.ds(chunk * 96, 96), :],
-                        up.at[chunk, pl.ds(pl.multiple_of(block * 96, 96), 96), :],
-                    )
-                )
+                target = up.at[chunk, pl.ds(pl.multiple_of(block * 96, 96), 96), :]
+                ups[chunk].append((piece.at[pl.ds(chunk * 96, 96), :], target))
         if first + size == 768:
-            copies.append(
-                (
-                    piece.at[pl.ds(384 - first, 384), :],
-                    down.at[pl.ds(pl.multiple_of(block * 384, 384), 384), :],
-                )
-            )
-    return started(copies, sems)
+            target = down.at[pl.ds(pl.multiple_of(block * 384, 384), 384), :]
+            downs.append((block, piece.at[pl.ds(384 - first, 384), :], target))
+    count = iter(range(40))
+    ups = [[pltpu.make_async_copy(a, b, sems.at[next(count)]) for a, b in each] for each in ups]
+    downs = [(k, pltpu.make_async_copy(a, b, sems.at[next(count)])) for k, a, b in downs]
+    return ups, downs
+
+
+def start_expert(copies):
+    ups, downs = copies
+    for copy in [*ups[0], *(copy for _, copy in downs), *ups[1], *ups[2], *ups[3]]:
+        copy.start()
+
+
+def wait_expert(copies, step):
+    ups, downs = copies
+    for chunk in range(4):
+        pl.when(step == chunk)(functools.partial(wait_all, ups[chunk]))
+    for block, copy in downs:
+        pl.when(block // 2 == step)(copy.wait)
 
 
 def wait_all(copies):
@@ -195,10 +204,12 @@
     blocks = where_ref[10]
     core = where_ref[8]
 
+    expert_loads = expert_copies(where_ref, pieces, w_up, w_down, sems)
+
     @pl.when(step == 0)
     def _():
         copies = load_pieces(where_ref, attention_pieces, w_out, attention_sems, (3 * D, D))
-        more = load_expert(where_ref, pieces, w_up, w_down, sems)
+        start_expert(expert_loads)
 
         def gather(block, _):
             pick, at = chosen(place, block), rows_of(block)
@@ -218,10 +229,23 @@
         lax.fori_loop(0, blocks, gather, 0)
         wait_all(copies)
         lax.fori_loop(0, blocks, norm, 0)
-        wait_all(more)
-
+
+    wait_expert(expert_loads, step)
     up = w_up.at[step]
     down = w_down.at[pl.ds(pl.multiple_of(step * D, D), D), :]
+
+    up_at = pl.ds(pl.multiple_of(step * 96, 96), 96)
+    mine = jnp.bitwise_xor(step, where_ref[9])
+
+    def put(down_grad, up_grad):
+        for block in range(8):
+            side = jnp.bitwise_xor(block & 1, core)
+            j = jnp.bitwise_xor(block >> 1, where_ref[9])
+            stage[side, j, up_at, :] = up_grad[block * 96 : (block + 1) * 96].astype(BF16)
+        for half in range(2):
+            side = jnp.bitwise_xor(half, core)
+            rows = down_grad[half * 384 : (half + 1) * 384]
+            stage[side, mine, pl.ds(384, 384), :] = rows.astype(BF16)
 
     def expert(block, _):
         at = rows_of(block)
@@ -232,18 +256,20 @@
         slope = chance + pre * (jnp.exp(-0.5 * pre * pre) * (1.0 / math.sqrt(2.0 * math.pi)))
         grad_pre = (dot_nt(grads, down[...]) * slope).astype(BF16)
         grad_two[at, :] += dot_nt(grad_pre, up[...])
-        add_down = dot_tn(activated, grads)
-        add_up = dot_tn(rows, grad_pre)
-
-        @pl.when(block == 0)
+
+        @pl.when(blocks == 1)
         def _():
-            sum_down[...] = add_down
-            sum_up[...] = add_up
+            put(dot_tn(activated, grads), dot_tn(rows, grad_pre))
+
+        @pl.when((blocks > 1) & (block == 0))
+        def _():
+            sum_down[...] = dot_tn(activated, grads)
+            sum_up[...] = dot_tn(rows, grad_pre)
 
         @pl.when(block > 0)
         def _():
-            sum_down[...] += add_down
-            sum_up[...] += add_up
+            sum_down[...] += dot_tn(activated, grads)
+            sum_up[...] += dot_tn(rows, grad_pre)
 
         return 0
 
@@ -272,15 +298,10 @@
             else:
                 pl.when(when)(functools.partial(act, copy))
 
-    up_at = pl.ds(pl.multiple_of(step * 96, 96), 96)
-    mine = jnp.bitwise_xor(step, where_ref[9])
-    for side in range(2):
-        for j in range(4):
-            source = pl.ds(pl.multiple_of(where_ref[4 * side + j] * 96, 96), 96)
-            stage[side, j, up_at, :] = sum_up[source, :].astype(BF16)
-        half = core if side == 0 else 1 - core
-        source = pl.ds(pl.multiple_of(half * 384, 384), 384)
-        stage[side, mine, pl.ds(384, 384), :] = sum_down[source, :].astype(BF16)
+    @pl.when(blocks > 1)
+    def _():
+        put(sum_down[...], sum_up[...])
+
     each(leaving(step), lambda copy: copy.start())
 
     @pl.when(step == pl.num_programs(0) - 1)
@@ -288,7 +309,7 @@
         sums[...] = jnp.zeros_like(sums)
 
         def back(block, _):
-            pick, at = chosen(place, block), rows_of(block)
+            at = rows_of(block)
             unit, inverse = normalize(rows_hidden[at, :])
             grad = grad_two[at, :]
             grad_hidden = rows_cot[at, :].astype(F32) + normalize_back(
@@ -298,19 +319,28 @@
             sums[1:2] += total(grad)
             sums[2:3] += total(grad_hidden)
             grad_attn = grad_hidden.astype(BF16)
-            add_out = dot_tn(rows_context[at, :], grad_attn)
-            rows = dot_nt(grad_attn, w_out[...]).astype(BF16)
-            rows = dot_tn(pick, rows).astype(BF16)
+            rows_two[at, :] = grad_attn
 
             @pl.when(block == 0)
             def _():
-                sum_up[...] = add_out
-                grad_context[...] = rows
+                sum_up[...] = dot_tn(rows_context[at, :], grad_attn)
 
             @pl.when(block > 0)
             def _():
-                sum_up[...] += add_out
-                grad_context[...] += rows
+                sum_up[...] += dot_tn(rows_context[at, :], grad_attn)
+
+            return 0
+
+        def spread(block, _):
+            rows = dot_nt(rows_two[rows_of(block), :], w_out[...]).astype(BF16)
+
+            @pl.when(block == 0)
+            def _():
+                grad_context[...] = dot_tn(chosen(place, block), rows).astype(BF16)
+
+            @pl.when(block > 0)
+            def _():
+                grad_context[...] += dot_tn(chosen(place, block), rows).astype(BF16)
 
             return 0
 
@@ -327,6 +357,7 @@
             (None, stage.at[1, 3, rows, :], send_far.at[rows, :], sem.at[2]),
         ]
         each(last, lambda copy: copy.start())
+        lax.fori_loop(0, blocks, spread, 0)
         each(last, lambda copy: copy.wait())
         for at_step in range(4):
             each(leaving(at_step), lambda copy: copy.wait())
@@ -438,10 +469,12 @@
     out, normed_two, w_up, w_down, w_out, sems, attention_sems, tails = rest
     step = pl.program_id(0)
 
+    expert_loads = expert_copies(where_ref, pieces, w_up, w_down, sems)
+
     @pl.when(step == 0)
     def _():
         copies = load_pieces(where_ref, attention_pieces, w_out, attention_sems, (3 * D, D))
-        more = load_expert(where_ref, pieces, w_up, w_down, sems)
+        start_expert(expert_loads)
         wait_all(copies)
         for seq in range(tokens.shape[0] // SEQ):
             at = pl.ds(seq * SEQ, SEQ)
@@ -452,8 +485,8 @@
             second = (unit * params[2:3] + params[3:4]).astype(BF16)
             normed_two[at, :] = second
             tails[pl.ds(seq * TAIL, TAIL), :] = second[HEAD:]
-        wait_all(more)
-
+
+    wait_expert(expert_loads, step)
     down = w_down.at[pl.ds(pl.multiple_of(step * D, D), D), :]
     feed(True, where_ref, normed_two, out, w_up.at[step], down, tails)
 
@@ -462,12 +495,14 @@
     pieces, (out, sums, w_up, w_down, sems, flat) = rest[:10], rest[10:]
     step = pl.program_id(0)
 
+    expert_loads = expert_copies(where_ref, pieces, w_up, w_down, sems)
+
     @pl.when(step == 0)
     def _():
-        copies = load_expert(where_ref, pieces, w_up, w_down, sems)
+        start_expert(expert_loads)
         sums[...] = before[...]
-        wait_all(copies)
-
+
+    wait_expert(expert_loads, step)
     down = w_down.at[pl.ds(pl.multiple_of(step * D, D), D), :]
     feed(False, where_ref, rows_in, sums, w_up.at[step], down, None)
 

time: 275 us -> 283 us (1.029)
  starting transfers between devices: 47.2 us -> 60.5 us
  waiting for transfers between devices: 54.9 us -> 51.1 us
    ppermute x15, starting transfers between devices: 22.8 us -> 36 us  [turn(): return lax.ppermute(block, 'z', [(i, (i + k) % 4) for i in range(4)])]
    ppermute x15, waiting for transfers between devices: 22.3 us -> 19.3 us  [turn(): return lax.ppermute(block, 'z', [(i, (i + k) % 4) for i in range(4)])]
  transfers between devices with their start and end apart: 50 -> 50, of which waited for: 14 -> 13; matrix products, arithmetic and copies ran while one was open for 14% -> 14% of each run, Pallas kernels for 41% -> 40%
where the time goes in v2:
time: 283 us; the launch traced here: 279 us
  Pallas kernels  111 us (39%)
  starting transfers between devices  60.5 us (21%)
  waiting for transfers between devices  51.1 us (18%)
  other arithmetic  28 us (10%)
  local copies, waits for them, and re-layouts  25.9 us (9%)
    pallas_call x5, Pallas kernels, call(): return run(*ins)  111 us
    ppermute x15, starting transfers between devices, turn(): return lax.ppermute(block, 'z', [(i, (i + k) % 4) for i in range(4)])  36 us
    ppermute x33, waiting for transfers between devices, swapped(): return lax.ppermute(block, axis, self.swap)  31.8 us
    ppermute x33, starting transfers between devices, swapped(): return lax.ppermute(block, axis, self.swap)  22.5 us
    ppermute x15, waiting for transfers between devices, turn(): return lax.ppermute(block, 'z', [(i, (i + k) % 4) for i in range(4)])  19.3 us
    reshape x2, local copies, waits for them, and re-layouts, lay(): rows = rows.reshape(seqs, LEN, -1)  5.73 us
  transfers between devices with their start and end apart: 50, of which 13 were waited for; matrix products, arithmetic and copies ran while one was open for 14% of the time, Pallas kernels for 40%

profile of v2, /device:TPU:16, one launch (start us, length us, event | category | flops | bytes accessed | tf_op | source)
XLA Modules:
  0.0 278.8 jit_solution(12837181165312503913)
XLA Ops:
  2.4 1.6 collective-permute-start
  4.4 1.2 collective-permute-start.2
  11.3 4.6 %collective-permute-done = bf16[24,3200]{1,0:T(8,128)(2,1)S(1)} collective-permute-done((bf16[24,3200]{1,0:T(8,128)(2,1)S(1)}, bf16[24,3200]{1,0:T(8,128)(2,1)S(1)}, u32[]{:S(2)}, u32[]{:S(2)}) %collective-permute-start) | collective-permute-done | bytes 153632 | tf_op jit(solution)/shard_map/ppermute | solution.py:582
  17.1 1.6 collective-permute-start.3
  19.0 1.6 collective-permute-start.4
  21.7 2.6 collective-permute-start.10
  24.3 1.3 collective-permute-start.11
  25.6 2.9 %reshape.298 = bf16[4,237,768]{2,1,0:T(8,128)(2,1)} reshape(bf16[948,768]{1,0:T(8,128)(2,1)} %param.13) | data formatting | bytes 2912256 | tf_op jit(solution)/shard_map/reshape | solution.py:546
  28.5 2.9 %reshape.300 = bf16[4,237,768]{2,1,0:T(8,128)(2,1)} reshape(bf16[948,768]{1,0:T(8,128)(2,1)} %param.16) | data formatting | bytes 2912256 | tf_op jit(solution)/shard_map/reshape | solution.py:546
  31.3 2.5 collective-permute-done.3.rest_1_.rest_11_
  33.9 2.5 collective-permute-start.12
  36.3 1.9 slice_select_fusion
  40.4 1.9 fusion.5
  42.2 5.5 %collective-permute-done.4.rest_2_.rest_12_ = bf16[96,3200]{1,0:T(8,128)(2,1)S(1)} collective-permute-done((bf16[96,3200]{1,0:T(8,128)(2,1)S(1)}, bf16[96,3200]{1,0:T(8,128)(2,1)S(1)}, u32[]{:S(2)}, u32[]{:S(2)}) %collective-permute-start.4) | collective-permute-done | bytes 614432 | tf_op jit(solution)/shard_map/ppermute | solution.py:601
  50.3 1.2 collective-permute-done.7.rest_5_.rest_15_
  53.4 1.4 collective-permute-start.14
  54.8 1.8 collective-permute-start.15
  56.6 2.2 collective-permute-start.16
  59.4 23.3 %attention.1 = (bf16[1024,2304]{1,0:T(8,128)(2,1)}, f32[4,6,256,512]{3,2,1,0:T(8,128)}, bf16[1024,768]{1,0:T(8,128)(2,1)}, bf16[1024,768]{1,0:T(8,128)(2,1)}, f32[8,768]{1,0:T(8,128)}) custom-call(s32[15]{0:T(128)} %concatenate.53.where_ref, bf16[1024,768]{1,0:T(8,128)(2,1)} %bitcast.145, f32[4,8,256]{2,1,0:T(8,128)} %broadcast_in_dim.4.masked, ...), custom_call_target="tpu_custom_call" | custom-call | flops 1 | bytes 1 | tf_op jit(solution)/shard_map/attention/pallas_call | solution.py:542
  85.3 1.3 select_bitcast_fusion.3
  88.0 10.9 %collective-permute-done.18.rest_3_ = bf16[384,768]{1,0:T(8,128)(2,1)S(1)} collective-permute-done((bf16[384,768]{1,0:T(8,128)(2,1)S(1)}, bf16[384,768]{1,0:T(8,128)(2,1)S(1)}, u32[]{:S(2)}, u32[]{:S(2)}) %collective-permute-start.18) | collective-permute-done | bytes 589856 | tf_op jit(solution)/shard_map/ppermute | solution.py:601
  100.3 1.5 collective-permute-start.21
  105.6 21.7 %feed_back.1 = (bf16[4,864,768]{2,1,0:T(8,128)(2,1)}, bf16[3,864,768]{2,1,0:T(8,128)(2,1)}, bf16[864,768]{1,0:T(8,128)(2,1)}, bf16[1024,768]{1,0:T(8,128)(2,1)}, f32[8,768]{1,0:T(8,128)}) custom-call(s32[15]{0:T(128)} %concatenate.53.where_ref, s32[1,1024]{1,0:T(1,128)} %get-tuple-element.175.place, f32[1,768]{1,0:T(1,128)} %reshape.341.vector, ...), custom_call_target="tpu_custom_call" | custom-call | flops 1 | bytes 1 | tf_op jit(solution)/shard_map/feed_back/pallas_call | solution.py:542
  127.8 1.9 slice.218
  129.7 1.9 slice.219
  131.7 2.7 fusion.7
  135.2 1.3 collective-permute-start.29
  137.2 1.3 collective-permute-start.32
  138.5 17.9 %feed_text.1 = (f32[1024,768]{1,0:T(8,128)}, bf16[1024,768]{1,0:T(8,128)(2,1)}) custom-call(s32[15]{0:T(128)} %concatenate.53.where_ref, bf16[1024,768]{1,0:T(8,128)(2,1)} %bitcast.146, f32[4,8,256]{2,1,0:T(8,128)} %broadcast_in_dim.4.masked, f32[1,768]{1,0:T(1,128)} %reshape.341.vector, bf16[1024,768]{1,0:T(8,128)(2,1)} %get-tuple-element.198.context, ...), custom_call_target="tpu_custom_call" | custom-call | flops 1 | bytes 1 | tf_op jit(solution)/shard_map/feed_text/pallas_call | solution.py:542
  156.4 8.7 %collective-permute-done.31.rest_3_ = bf16[384,768]{1,0:T(8,128)(2,1)} collective-permute-done((bf16[384,768]{1,0:T(8,128)(2,1)}, bf16[384,768]{1,0:T(8,128)(2,1)}, u32[]{:S(2)}, u32[]{:S(2)}) %collective-permute-start.31) | collective-permute-done | bytes 589856 | tf_op jit(solution)/shard_map/ppermute | solution.py:601
  165.8 5.2 %fusion.3 = (bf16[864,768]{1,0:T(8,128)(2,1)}, bf16[864,768]{1,0:T(8,128)(2,1)}) fusion(bf16[432,768]{1,0:T(8,128)(2,1)} %collective-permute-done.28, bf16[3,864,768]{2,1,0:T(8,128)(2,1)S(1)} %collective-permute-done.30, bf16[4,864,768]{2,1,0:T(8,128)(2,1)} %get-tuple-element.221, bf16[432,768]{1,0:T(8,128)(2,1)} %collective-permute-done.29), kind=kLoop, calls=%fused_computation.6 | loop fusion | flops 7962624 | bytes 9289728 | tf_op jit(solution)/shard_map/convert_element_type | solution.py:645
  171.8 1.3 collective-permute-start.35
  174.4 30.4 %attention_back.1 = (bf16[4,304,768]{2,1,0:T(8,128)(2,1)}, bf16[4,304,768]{2,1,0:T(8,128)(2,1)}, f32[948,768]{1,0:T(8,128)}) custom-call(s32[15]{0:T(128)} %concatenate.53.where_ref, bf16[1024,2304]{1,0:T(8,128)(2,1)} %get-tuple-element.166.qkv, f32[4,6,256,512]{3,2,1,0:T(8,128)} %get-tuple-element.167.softs, ...), custom_call_target="tpu_custom_call" | custom-call | flops 1 | bytes 1 | tf_op jit(solution)/shard_map/attention_back/pallas_call | solution.py:542
  205.5 2.4 fusion.18
  210.7 1.3 copy-done.19
  212.0 1.3 fusion.13
  214.0 1.2 collective-permute-start.42
  215.2 1.6 collective-permute-start.43
  216.7 2.0 collective-permute-start.44
  218.7 11.8 %collective-permute-start.45 = (bf16[216,768]{1,0:T(8,128)(2,1)}, bf16[216,768]{1,0:T(8,128)(2,1)}, u32[]{:S(2)}, u32[]{:S(2)}) collective-permute-start(bf16[216,768]{1,0:T(8,128)(2,1)} %pad_maximum_fusion.7), channel_id=1, source_target_pairs={{0,2},{1,3},{2,0},{3,1},{4,6},{5,7},{6,4},{7,5},{8,10},{9,11},{10,... | collective-permute-start | bytes 995336 | tf_op jit(solution)/shard_map/ppermute | solution.py:582
  230.6 17.5 %feed_image.1 = bf16[948,768]{1,0:T(8,128)(2,1)} custom-call(s32[15]{0:T(128)} %concatenate.53.where_ref, bf16[1024,768]{1,0:T(8,128)(2,1)} %get-tuple-element.240.rows_in, f32[1024,768]{1,0:T(8,128)} %get-tuple-element.241.before, bf16[768,768]{1,0:T(8,128)(2,1)} %pad_maximum_fusion.3.rest_0_, bf16[768,768]{1,0:T(8,128)(2,1)} %collective-permute-done.20.rest_1_, ...), custom_call_target="tpu_custom_call" | custom-call | flops 1 | bytes 1 | tf_op jit(solution)/shard_map/feed_image/pallas_call | solution.py:542
  248.9 1.6 fusion.16
  250.6 2.3 collective-permute-start.48
  252.9 4.3 %collective-permute-start.47 = (bf16[80,768]{1,0:T(8,128)(2,1)S(1)}, bf16[80,768]{1,0:T(8,128)(2,1)S(1)}, u32[]{:S(2)}, u32[]{:S(2)}) collective-permute-start(bf16[80,768]{1,0:T(8,128)(2,1)S(1)} %get-tuple-element.317), channel_id=1, source_target_pairs={{0,2},{1,3},{2,0},{3,1},{4,6},{5,7},{6,4},{7,5},{8,10},{9,11},{10,... | collective-permute-start | bytes 368648 | tf_op jit(solution)/shard_map/ppermute | solution.py:582
  257.2 2.1 collective-permute-start.49
  259.3 4.7 %collective-permute-done.47 = bf16[80,768]{1,0:T(8,128)(2,1)S(1)} collective-permute-done((bf16[80,768]{1,0:T(8,128)(2,1)S(1)}, bf16[80,768]{1,0:T(8,128)(2,1)S(1)}, u32[]{:S(2)}, u32[]{:S(2)}) %collective-permute-start.47) | collective-permute-done | bytes 122912 | tf_op jit(solution)/shard_map/ppermute | solution.py:582
  264.0 9.1 %collective-permute-done.46 = bf16[80,768]{1,0:T(8,128)(2,1)S(1)} collective-permute-done((bf16[80,768]{1,0:T(8,128)(2,1)S(1)}, bf16[80,768]{1,0:T(8,128)(2,1)S(1)}, u32[]{:S(2)}, u32[]{:S(2)}) %collective-permute-start.46) | collective-permute-done | bytes 122912 | tf_op jit(solution)/shard_map/ppermute | solution.py:582
  275.2 1.2 add_add_fusion
  (204 shorter events, 39.9 us)
Async XLA Ops:
  2.4 13.5 %collective-permute-start = (bf16[24,3200]{1,0:T(8,128)(2,1)S(1)}, bf16[24,3200]{1,0:T(8,128)(2,1)S(1)}, u32[]{:S(2)}, u32[]{:S(2)}) collective-permute-start(bf16[24,3200]{1,0:T(8,128)(2,1)S(1)} %fusion.15), channel_id=1, source_target_pairs={{0,1},{1,2},{2,3},{3,0},{4,5},{5,6},{6,7},{7,4},{8,9},{9,10},{10,1... | collective-permute-start | bytes 460808 | tf_op jit(solution)/shard_map/ppermute | solution.py:582
  4.0 11.9 %collective-permute-start.1 = (bf16[24,3200]{1,0:T(8,128)(2,1)S(1)}, bf16[24,3200]{1,0:T(8,128)(2,1)S(1)}, u32[]{:S(2)}, u32[]{:S(2)}) collective-permute-start(bf16[24,3200]{1,0:T(8,128)(2,1)S(1)} %fusion.15), channel_id=1, source_target_pairs={{0,2},{1,3},{2,0},{3,1},{4,6},{5,7},{6,4},{7,5},{8,10},{9,11},{10,... | collective-permute-start | bytes 460808 | tf_op jit(solution)/shard_map/ppermute | solution.py:582
  4.4 12.5 %collective-permute-start.2 = (bf16[24,3200]{1,0:T(8,128)(2,1)S(1)}, bf16[24,3200]{1,0:T(8,128)(2,1)S(1)}, u32[]{:S(2)}, u32[]{:S(2)}) collective-permute-start(bf16[24,3200]{1,0:T(8,128)(2,1)S(1)} %fusion.15), channel_id=1, source_target_pairs={{0,3},{1,0},{2,1},{3,2},{4,7},{5,4},{6,5},{7,6},{8,11},{9,8},{10,9... | collective-permute-start | bytes 460808 | tf_op jit(solution)/shard_map/ppermute | solution.py:582
  17.1 16.8 %collective-permute-start.3 = (bf16[96,3200]{1,0:T(8,128)(2,1)S(1)}, bf16[96,3200]{1,0:T(8,128)(2,1)S(1)}, u32[]{:S(2)}, u32[]{:S(2)}) collective-permute-start(bf16[96,3200]{1,0:T(8,128)(2,1)S(1)} %bitcast.148), channel_id=1, source_target_pairs={{0,8},{8,0},{1,9},{9,1},{2,10},{10,2},{3,11},{11,3},{4,12},{12,4},... | collective-permute-start | bytes 1843208 | tf_op jit(solution)/shard_map/ppermute | solution.py:601
  19.0 28.7 %collective-permute-start.4 = (bf16[96,3200]{1,0:T(8,128)(2,1)S(1)}, bf16[96,3200]{1,0:T(8,128)(2,1)S(1)}, u32[]{:S(2)}, u32[]{:S(2)}) collective-permute-start(bf16[96,3200]{1,0:T(8,128)(2,1)S(1)} %bitcast.149), channel_id=1, source_target_pairs={{0,16},{16,0},{1,17},{17,1},{2,18},{18,2},{3,19},{19,3},{4,20},{20... | collective-permute-start | bytes 1843208 | tf_op jit(solution)/shard_map/ppermute | solution.py:601
  20.6 27.1 %collective-permute-start.5 = (bf16[96,3200]{1,0:T(8,128)(2,1)S(1)}, bf16[96,3200]{1,0:T(8,128)(2,1)}, u32[]{:S(2)}, u32[]{:S(2)}) collective-permute-start(bf16[96,3200]{1,0:T(8,128)(2,1)S(1)} %bitcast.150), channel_id=1, source_target_pairs={{0,24},{8,16},{16,8},{24,0},{1,25},{9,17},{17,9},{25,1},{2,26},{10... | collective-permute-start | bytes 1843208 | tf_op jit(solution)/shard_map/ppermute | solution.py:624
  21.7 26.6 %collective-permute-start.10 = (bf16[192,768]{1,0:T(8,128)(2,1)S(1)}, bf16[192,768]{1,0:T(8,128)(2,1)S(1)}, u32[]{:S(2)}, u32[]{:S(2)}) collective-permute-start(bf16[192,768]{1,0:T(8,128)(2,1)S(1)} %pad_maximum_fusion.9), channel_id=1, source_target_pairs={{0,1},{1,2},{2,3},{3,0},{4,5},{5,6},{6,7},{7,4},{8,9},{9,10},{10,1... | collective-permute-start | bytes 884744 | tf_op jit(solution)/shard_map/ppermute | solution.py:582
  24.3 24.1 %collective-permute-start.11 = (bf16[192,768]{1,0:T(8,128)(2,1)S(1)}, bf16[192,768]{1,0:T(8,128)(2,1)}, u32[]{:S(2)}, u32[]{:S(2)}) collective-permute-start(bf16[192,768]{1,0:T(8,128)(2,1)S(1)} %pad_maximum_fusion.9), channel_id=1, source_target_pairs={{0,2},{1,3},{2,0},{3,1},{4,6},{5,7},{6,4},{7,5},{8,10},{9,11},{10,... | collective-permute-start | bytes 884744 | tf_op jit(solution)/shard_map/ppermute | solution.py:582
  33.9 15.0 %collective-permute-start.12 = (bf16[192,768]{1,0:T(8,128)(2,1)S(1)}, bf16[192,768]{1,0:T(8,128)(2,1)S(1)}, u32[]{:S(2)}, u32[]{:S(2)}) collective-permute-start(bf16[192,768]{1,0:T(8,128)(2,1)S(1)} %pad_maximum_fusion.9), channel_id=1, source_target_pairs={{0,3},{1,0},{2,1},{3,2},{4,7},{5,4},{6,5},{7,6},{8,11},{9,8},{10,9... | collective-permute-start | bytes 884744 | tf_op jit(solution)/shard_map/ppermute | solution.py:582
  47.8 3.8 %collective-permute-start.7 = (bf16[96,3200]{1,0:T(8,128)(2,1)S(1)}, bf16[96,3200]{1,0:T(8,128)(2,1)S(1)}, u32[]{:S(2)}, u32[]{:S(2)}) collective-permute-start(bf16[96,3200]{1,0:T(8,128)(2,1)S(1)} %collective-permute-done.3.rest_1_.rest_11_), channel_id=1, source_target_pairs={{0,4},{4,0},{1,5},{5,1},{2,6},{6,2},{3,7},{7,3},{8,12},{12,8},{9,1... | collective-permute-start | bytes 1843208 | tf_op jit(solution)/shard_map/ppermute | solution.py:601
  48.3 4.2 %collective-permute-start.8 = (bf16[96,3200]{1,0:T(8,128)(2,1)S(1)}, bf16[96,3200]{1,0:T(8,128)(2,1)S(1)}, u32[]{:S(2)}, u32[]{:S(2)}) collective-permute-start(bf16[96,3200]{1,0:T(8,128)(2,1)S(1)} %collective-permute-done.4.rest_2_.rest_12_), channel_id=1, source_target_pairs={{0,4},{4,0},{1,5},{5,1},{2,6},{6,2},{3,7},{7,3},{8,12},{12,8},{9,1... | collective-permute-start | bytes 1843208 | tf_op jit(solution)/shard_map/ppermute | solution.py:601
  48.4 4.1 %collective-permute-start.9 = (bf16[96,3200]{1,0:T(8,128)(2,1)}, bf16[96,3200]{1,0:T(8,128)(2,1)S(1)}, u32[]{:S(2)}, u32[]{:S(2)}) collective-permute-start(bf16[96,3200]{1,0:T(8,128)(2,1)} %collective-permute-done.5.rest_3_.rest_13_), channel_id=1, source_target_pairs={{0,4},{4,0},{1,5},{5,1},{2,6},{6,2},{3,7},{7,3},{8,12},{12,8},{9,1... | collective-permute-start | bytes 1843208 | tf_op jit(solution)/shard_map/ppermute | solution.py:601
  52.5 30.3 %collective-permute-start.13 = (bf16[768,768]{1,0:T(8,128)(2,1)S(1)}, bf16[768,768]{1,0:T(8,128)(2,1)S(1)}, u32[]{:S(2)}, u32[]{:S(2)}) collective-permute-start(bf16[768,768]{1,0:T(8,128)(2,1)S(1)} %pad_maximum_fusion.1.rest_0_), channel_id=1, source_target_pairs={{0,8},{8,0},{1,9},{9,1},{2,10},{10,2},{3,11},{11,3},{4,12},{12,4},... | collective-permute-start | bytes 3538952 | tf_op jit(solution)/shard_map/ppermute | solution.py:601
  53.4 29.4 %collective-permute-start.14 = (bf16[768,768]{1,0:T(8,128)(2,1)S(1)}, bf16[768,768]{1,0:T(8,128)(2,1)S(1)}, u32[]{:S(2)}, u32[]{:S(2)}) collective-permute-start(bf16[768,768]{1,0:T(8,128)(2,1)S(1)} %pad_maximum_fusion.1.rest_0_), channel_id=1, source_target_pairs={{0,16},{16,0},{1,17},{17,1},{2,18},{18,2},{3,19},{19,3},{4,20},{20... | collective-permute-start | bytes 3538952 | tf_op jit(solution)/shard_map/ppermute | solution.py:601
  54.8 27.9 %collective-permute-start.15 = (bf16[192,768]{1,0:T(8,128)(2,1)S(1)}, bf16[192,768]{1,0:T(8,128)(2,1)}, u32[]{:S(2)}, u32[]{:S(2)}) collective-permute-start(bf16[192,768]{1,0:T(8,128)(2,1)S(1)} %pad_maximum_fusion.10), channel_id=1, source_target_pairs={{0,1},{1,2},{2,3},{3,0},{4,5},{5,6},{6,7},{7,4},{8,9},{9,10},{10,1... | collective-permute-start | bytes 884744 | tf_op jit(solution)/shard_map/ppermute | solution.py:582
  56.6 26.1 %collective-permute-start.16 = (bf16[192,768]{1,0:T(8,128)(2,1)S(1)}, bf16[192,768]{1,0:T(8,128)(2,1)}, u32[]{:S(2)}, u32[]{:S(2)}) collective-permute-start(bf16[192,768]{1,0:T(8,128)(2,1)S(1)} %pad_maximum_fusion.10), channel_id=1, source_target_pairs={{0,2},{1,3},{2,0},{3,1},{4,6},{5,7},{6,4},{7,5},{8,10},{9,11},{10,... | collective-permute-start | bytes 884744 | tf_op jit(solution)/shard_map/ppermute | solution.py:582
  58.8 24.0 %collective-permute-start.17 = (bf16[192,768]{1,0:T(8,128)(2,1)S(1)}, bf16[192,768]{1,0:T(8,128)(2,1)}, u32[]{:S(2)}, u32[]{:S(2)}) collective-permute-start(bf16[192,768]{1,0:T(8,128)(2,1)S(1)} %pad_maximum_fusion.10), channel_id=1, source_target_pairs={{0,3},{1,0},{2,1},{3,2},{4,7},{5,4},{6,5},{7,6},{8,11},{9,8},{10,9... | collective-permute-start | bytes 884744 | tf_op jit(solution)/shard_map/ppermute | solution.py:582
  82.8 19.0 %collective-permute-start.23 = (bf16[768,768]{1,0:T(8,128)(2,1)S(1)}, bf16[768,768]{1,0:T(8,128)(2,1)S(1)}, u32[]{:S(2)}, u32[]{:S(2)}) collective-permute-start(bf16[768,768]{1,0:T(8,128)(2,1)S(1)} %collective-permute-done.13.rest_1_), channel_id=1, source_target_pairs={{0,4},{4,0},{1,5},{5,1},{2,6},{6,2},{3,7},{7,3},{8,12},{12,8},{9,1... | collective-permute-start | bytes 3538952 | tf_op jit(solution)/shard_map/ppermute | solution.py:601
  83.0 19.4 %collective-permute-start.24 = (bf16[768,768]{1,0:T(8,128)(2,1)S(1)}, bf16[768,768]{1,0:T(8,128)(2,1)S(1)}, u32[]{:S(2)}, u32[]{:S(2)}) collective-permute-start(bf16[768,768]{1,0:T(8,128)(2,1)S(1)} %collective-permute-done.14.rest_2_), channel_id=1, source_target_pairs={{0,4},{4,0},{1,5},{5,1},{2,6},{6,2},{3,7},{7,3},{8,12},{12,8},{9,1... | collective-permute-start | bytes 3538952 | tf_op jit(solution)/shard_map/ppermute | solution.py:601
  83.5 15.3 %collective-permute-start.18 = (bf16[384,768]{1,0:T(8,128)(2,1)S(1)}, bf16[384,768]{1,0:T(8,128)(2,1)S(1)}, u32[]{:S(2)}, u32[]{:S(2)}) collective-permute-start(bf16[384,768]{1,0:T(8,128)(2,1)S(1)} %slice.210), channel_id=1, source_target_pairs={{0,16},{16,0},{1,17},{17,1},{2,18},{18,2},{3,19},{19,3},{4,20},{20... | collective-permute-start | bytes 1769480 | tf_op jit(solution)/shard_map/ppermute | solution.py:601
  84.1 15.0 %collective-permute-start.19 = (bf16[384,768]{1,0:T(8,128)(2,1)S(1)}, bf16[384,768]{1,0:T(8,128)(2,1)S(1)}, u32[]{:S(2)}, u32[]{:S(2)}) collective-permute-start(bf16[384,768]{1,0:T(8,128)(2,1)S(1)} %slice.211), channel_id=1, source_target_pairs={{0,8},{8,0},{1,9},{9,1},{2,10},{10,2},{3,11},{11,3},{4,12},{12,4},... | collective-permute-start | bytes 1769480 | tf_op jit(solution)/shard_map/ppermute | solution.py:601
  85.3 16.6 %collective-permute-start.22 = (bf16[768,768]{1,0:T(8,128)(2,1)S(1)}, bf16[768,768]{1,0:T(8,128)(2,1)S(1)}, u32[]{:S(2)}, u32[]{:S(2)}) collective-permute-start(bf16[768,768]{1,0:T(8,128)(2,1)S(1)} %pad_maximum_fusion.1.rest_0_), channel_id=1, source_target_pairs={{0,4},{4,0},{1,5},{5,1},{2,6},{6,2},{3,7},{7,3},{8,12},{12,8},{9,1... | collective-permute-start | bytes 3538952 | tf_op jit(solution)/shard_map/ppermute | solution.py:601
  99.2 28.1 %collective-permute-start.20 = (bf16[768,768]{1,0:T(8,128)(2,1)}, bf16[768,768]{1,0:T(8,128)(2,1)}, u32[]{:S(2)}, u32[]{:S(2)}) collective-permute-start(bf16[768,768]{1,0:T(8,128)(2,1)} %pad_maximum_fusion.3.rest_0_), channel_id=1, source_target_pairs={{0,8},{8,0},{1,9},{9,1},{2,10},{10,2},{3,11},{11,3},{4,12},{12,4},... | collective-permute-start | bytes 3538952 | tf_op jit(solution)/shard_map/ppermute | solution.py:601
  100.3 27.0 %collective-permute-start.21 = (bf16[768,768]{1,0:T(8,128)(2,1)}, bf16[768,768]{1,0:T(8,128)(2,1)}, u32[]{:S(2)}, u32[]{:S(2)}) collective-permute-start(bf16[768,768]{1,0:T(8,128)(2,1)} %pad_maximum_fusion.3.rest_0_), channel_id=1, source_target_pairs={{0,16},{16,0},{1,17},{17,1},{2,18},{18,2},{3,19},{19,3},{4,20},{20... | collective-permute-start | bytes 3538952 | tf_op jit(solution)/shard_map/ppermute | solution.py:601
  101.9 2.8 %collective-permute-start.26 = (bf16[384,768]{1,0:T(8,128)(2,1)S(1)}, bf16[384,768]{1,0:T(8,128)(2,1)S(1)}, u32[]{:S(2)}, u32[]{:S(2)}) collective-permute-start(bf16[384,768]{1,0:T(8,128)(2,1)S(1)} %collective-permute-done.19.rest_4_), channel_id=1, source_target_pairs={{0,4},{4,0},{1,5},{5,1},{2,6},{6,2},{3,7},{7,3},{8,12},{12,8},{9,1... | collective-permute-start | bytes 1769480 | tf_op jit(solution)/shard_map/ppermute | solution.py:601
  127.3 4.4 %collective-permute-start.27 = (bf16[864,768]{1,0:T(8,128)(2,1)}, bf16[864,768]{1,0:T(8,128)(2,1)S(1)}, u32[]{:S(2)}, u32[]{:S(2)}) collective-permute-start(bf16[864,768]{1,0:T(8,128)(2,1)} %get-tuple-element.188), channel_id=1, source_target_pairs={{0,4},{4,0},{1,5},{5,1},{2,6},{6,2},{3,7},{7,3},{8,12},{12,8},{9,1... | collective-permute-start | bytes 3981320 | tf_op jit(solution)/shard_map/ppermute | solution.py:601
  134.4 30.8 %collective-permute-start.30 = (bf16[3,864,768]{2,1,0:T(8,128)(2,1)}, bf16[3,864,768]{2,1,0:T(8,128)(2,1)S(1)}, u32[]{:S(2)}, u32[]{:S(2)}) collective-permute-start(bf16[3,864,768]{2,1,0:T(8,128)(2,1)} %get-tuple-element.194), channel_id=1, source_target_pairs={{0,4},{4,0},{1,5},{5,1},{2,6},{6,2},{3,7},{7,3},{8,12},{12,8},{9,1... | collective-permute-start | bytes 11943944 | tf_op jit(solution)/shard_map/ppermute | solution.py:601
  134.4 30.7 %collective-permute-start.28 = (bf16[432,768]{1,0:T(8,128)(2,1)}, bf16[432,768]{1,0:T(8,128)(2,1)}, u32[]{:S(2)}, u32[]{:S(2)}) collective-permute-start(bf16[432,768]{1,0:T(8,128)(2,1)} %get-tuple-element.192), channel_id=1, source_target_pairs={{0,8},{8,0},{1,9},{9,1},{2,10},{10,2},{3,11},{11,3},{4,12},{12,4},... | collective-permute-start | bytes 1990664 | tf_op jit(solution)/shard_map/ppermute | solution.py:601
  135.2 30.0 %collective-permute-start.29 = (bf16[432,768]{1,0:T(8,128)(2,1)}, bf16[432,768]{1,0:T(8,128)(2,1)}, u32[]{:S(2)}, u32[]{:S(2)}) collective-permute-start(bf16[432,768]{1,0:T(8,128)(2,1)} %get-tuple-element.193), channel_id=1, source_target_pairs={{0,16},{16,0},{1,17},{17,1},{2,18},{18,2},{3,19},{19,3},{4,20},{20... | collective-permute-start | bytes 1990664 | tf_op jit(solution)/shard_map/ppermute | solution.py:601
  136.5 28.6 %collective-permute-start.31 = (bf16[384,768]{1,0:T(8,128)(2,1)}, bf16[384,768]{1,0:T(8,128)(2,1)}, u32[]{:S(2)}, u32[]{:S(2)}) collective-permute-start(bf16[384,768]{1,0:T(8,128)(2,1)} %slice.218), channel_id=1, source_target_pairs={{0,16},{16,0},{1,17},{17,1},{2,18},{18,2},{3,19},{19,3},{4,20},{20... | collective-permute-start | bytes 1769480 | tf_op jit(solution)/shard_map/ppermute | solution.py:601
  137.2 27.9 %collective-permute-start.32 = (bf16[384,768]{1,0:T(8,128)(2,1)}, bf16[384,768]{1,0:T(8,128)(2,1)}, u32[]{:S(2)}, u32[]{:S(2)}) collective-permute-start(bf16[384,768]{1,0:T(8,128)(2,1)} %slice.219), channel_id=1, source_target_pairs={{0,8},{8,0},{1,9},{9,1},{2,10},{10,2},{3,11},{11,3},{4,12},{12,4},... | collective-permute-start | bytes 1769480 | tf_op jit(solution)/shard_map/ppermute | solution.py:601
  165.2 5.8 %collective-permute-start.33 = (bf16[384,768]{1,0:T(8,128)(2,1)}, bf16[384,768]{1,0:T(8,128)(2,1)S(1)}, u32[]{:S(2)}, u32[]{:S(2)}) collective-permute-start(bf16[384,768]{1,0:T(8,128)(2,1)} %collective-permute-done.31.rest_3_), channel_id=1, source_target_pairs={{0,4},{4,0},{1,5},{5,1},{2,6},{6,2},{3,7},{7,3},{8,12},{12,8},{9,1... | collective-permute-start | bytes 1769480 | tf_op jit(solution)/shard_map/ppermute | solution.py:601
  165.3 5.7 %collective-permute-start.34 = (bf16[384,768]{1,0:T(8,128)(2,1)}, bf16[384,768]{1,0:T(8,128)(2,1)S(1)}, u32[]{:S(2)}, u32[]{:S(2)}) collective-permute-start(bf16[384,768]{1,0:T(8,128)(2,1)} %collective-permute-done.32.rest_4_), channel_id=1, source_target_pairs={{0,4},{4,0},{1,5},{5,1},{2,6},{6,2},{3,7},{7,3},{8,12},{12,8},{9,1... | collective-permute-start | bytes 1769480 | tf_op jit(solution)/shard_map/ppermute | solution.py:601
  171.8 33.1 %collective-permute-start.35 = (bf16[864,768]{1,0:T(8,128)(2,1)}, bf16[864,768]{1,0:T(8,128)(2,1)S(1)}, u32[]{:S(2)}, u32[]{:S(2)}) collective-permute-start(bf16[864,768]{1,0:T(8,128)(2,1)} %get-tuple-element.214), channel_id=1, source_target_pairs={{0,8},{8,0},{1,9},{9,1},{2,10},{10,2},{3,11},{11,3},{4,12},{12,4},... | collective-permute-start | bytes 3981320 | tf_op jit(solution)/shard_map/ppermute | solution.py:601
  173.0 31.8 %collective-permute-start.36 = (bf16[864,768]{1,0:T(8,128)(2,1)}, bf16[864,768]{1,0:T(8,128)(2,1)S(1)}, u32[]{:S(2)}, u32[]{:S(2)}) collective-permute-start(bf16[864,768]{1,0:T(8,128)(2,1)} %get-tuple-element.215), channel_id=1, source_target_pairs={{0,16},{16,0},{1,17},{17,1},{2,18},{18,2},{3,19},{19,3},{4,20},{20... | collective-permute-start | bytes 3981320 | tf_op jit(solution)/shard_map/ppermute | solution.py:601
  173.9 30.9 %collective-permute-start.37 = (bf16[768,768]{1,0:T(8,128)(2,1)}, bf16[768,768]{1,0:T(8,128)(2,1)}, u32[]{:S(2)}, u32[]{:S(2)}) collective-permute-start(bf16[768,768]{1,0:T(8,128)(2,1)} %pad_maximum_fusion.3.rest_0_), channel_id=1, source_target_pairs={{0,4},{4,0},{1,5},{5,1},{2,6},{6,2},{3,7},{7,3},{8,12},{12,8},{9,1... | collective-permute-start | bytes 3538952 | tf_op jit(solution)/shard_map/ppermute | solution.py:601
  173.9 31.0 %collective-permute-start.38 = (bf16[768,768]{1,0:T(8,128)(2,1)}, bf16[768,768]{1,0:T(8,128)(2,1)}, u32[]{:S(2)}, u32[]{:S(2)}) collective-permute-start(bf16[768,768]{1,0:T(8,128)(2,1)} %collective-permute-done.20.rest_1_), channel_id=1, source_target_pairs={{0,4},{4,0},{1,5},{5,1},{2,6},{6,2},{3,7},{7,3},{8,12},{12,8},{9,1... | collective-permute-start | bytes 3538952 | tf_op jit(solution)/shard_map/ppermute | solution.py:601
  174.4 30.5 %collective-permute-start.39 = (bf16[768,768]{1,0:T(8,128)(2,1)}, bf16[768,768]{1,0:T(8,128)(2,1)}, u32[]{:S(2)}, u32[]{:S(2)}) collective-permute-start(bf16[768,768]{1,0:T(8,128)(2,1)} %collective-permute-done.21.rest_2_), channel_id=1, source_target_pairs={{0,4},{4,0},{1,5},{5,1},{2,6},{6,2},{3,7},{7,3},{8,12},{12,8},{9,1... | collective-permute-start | bytes 3538952 | tf_op jit(solution)/shard_map/ppermute | solution.py:601
  204.9 5.8 %collective-permute-start.40 = (bf16[4,304,768]{2,1,0:T(8,128)(2,1)}, bf16[4,304,768]{2,1,0:T(8,128)(2,1)S(1)}, u32[]{:S(2)}, u32[]{:S(2)}) collective-permute-start(bf16[4,304,768]{2,1,0:T(8,128)(2,1)} %get-tuple-element.220), channel_id=1, source_target_pairs={{0,4},{4,0},{1,5},{5,1},{2,6},{6,2},{3,7},{7,3},{8,12},{12,8},{9,1... | collective-permute-start | bytes 5603336 | tf_op jit(solution)/shard_map/ppermute | solution.py:601
  213.2 34.9 %collective-permute-start.41 = (bf16[296,768]{1,0:T(8,128)(2,1)}, bf16[296,768]{1,0:T(8,128)(2,1)S(1)}, u32[]{:S(2)}, u32[]{:S(2)}) collective-permute-start(bf16[296,768]{1,0:T(8,128)(2,1)} %get-tuple-element.233), channel_id=1, source_target_pairs={{0,8},{8,0},{1,9},{9,1},{2,10},{10,2},{3,11},{11,3},{4,12},{12,4},... | collective-permute-start | bytes 1363976 | tf_op jit(solution)/shard_map/ppermute | solution.py:601
  214.0 34.1 %collective-permute-start.42 = (bf16[296,768]{1,0:T(8,128)(2,1)}, bf16[296,768]{1,0:T(8,128)(2,1)S(1)}, u32[]{:S(2)}, u32[]{:S(2)}) collective-permute-start(bf16[296,768]{1,0:T(8,128)(2,1)} %get-tuple-element.234), channel_id=1, source_target_pairs={{0,16},{16,0},{1,17},{17,1},{2,18},{18,2},{3,19},{19,3},{4,20},{20... | collective-permute-start | bytes 1363976 | tf_op jit(solution)/shard_map/ppermute | solution.py:601
  215.2 33.7 %collective-permute-start.43 = (bf16[296,768]{1,0:T(8,128)(2,1)S(1)}, bf16[296,768]{1,0:T(8,128)(2,1)}, u32[]{:S(2)}, u32[]{:S(2)}) collective-permute-start(bf16[296,768]{1,0:T(8,128)(2,1)S(1)} %get-tuple-element.235), channel_id=1, source_target_pairs={{0,24},{8,16},{16,8},{24,0},{1,25},{9,17},{17,9},{25,1},{2,26},{10... | collective-permute-start | bytes 1363976 | tf_op jit(solution)/shard_map/ppermute | solution.py:624
  216.7 31.4 %collective-permute-start.44 = (bf16[216,768]{1,0:T(8,128)(2,1)}, bf16[216,768]{1,0:T(8,128)(2,1)}, u32[]{:S(2)}, u32[]{:S(2)}) collective-permute-start(bf16[216,768]{1,0:T(8,128)(2,1)} %pad_maximum_fusion.6), channel_id=1, source_target_pairs={{0,1},{1,2},{2,3},{3,0},{4,5},{5,6},{6,7},{7,4},{8,9},{9,10},{10,1... | collective-permute-start | bytes 995336 | tf_op jit(solution)/shard_map/ppermute | solution.py:582
  218.7 29.4 %collective-permute-start.45 = (bf16[216,768]{1,0:T(8,128)(2,1)}, bf16[216,768]{1,0:T(8,128)(2,1)}, u32[]{:S(2)}, u32[]{:S(2)}) collective-permute-start(bf16[216,768]{1,0:T(8,128)(2,1)} %pad_maximum_fusion.7), channel_id=1, source_target_pairs={{0,2},{1,3},{2,0},{3,1},{4,6},{5,7},{6,4},{7,5},{8,10},{9,11},{10,... | collective-permute-start | bytes 995336 | tf_op jit(solution)/shard_map/ppermute | solution.py:582
  250.6 8.7 %collective-permute-start.48 = (bf16[80,768]{1,0:T(8,128)(2,1)S(1)}, bf16[80,768]{1,0:T(8,128)(2,1)S(1)}, u32[]{:S(2)}, u32[]{:S(2)}) collective-permute-start(bf16[80,768]{1,0:T(8,128)(2,1)S(1)} %get-tuple-element.318), channel_id=1, source_target_pairs={{0,3},{1,0},{2,1},{3,2},{4,7},{5,4},{6,5},{7,6},{8,11},{9,8},{10,9... | collective-permute-start | bytes 368648 | tf_op jit(solution)/shard_map/ppermute | solution.py:582
  252.9 11.1 %collective-permute-start.47 = (bf16[80,768]{1,0:T(8,128)(2,1)S(1)}, bf16[80,768]{1,0:T(8,128)(2,1)S(1)}, u32[]{:S(2)}, u32[]{:S(2)}) collective-permute-start(bf16[80,768]{1,0:T(8,128)(2,1)S(1)} %get-tuple-element.317), channel_id=1, source_target_pairs={{0,2},{1,3},{2,0},{3,1},{4,6},{5,7},{6,4},{7,5},{8,10},{9,11},{10,... | collective-permute-start | bytes 368648 | tf_op jit(solution)/shard_map/ppermute | solution.py:582
  257.1 15.9 %collective-permute-start.46 = (bf16[80,768]{1,0:T(8,128)(2,1)S(1)}, bf16[80,768]{1,0:T(8,128)(2,1)S(1)}, u32[]{:S(2)}, u32[]{:S(2)}) collective-permute-start(bf16[80,768]{1,0:T(8,128)(2,1)S(1)} %get-tuple-element.316), channel_id=1, source_target_pairs={{0,1},{1,2},{2,3},{3,0},{4,5},{5,6},{6,7},{7,4},{8,9},{9,10},{10,1... | collective-permute-start | bytes 368648 | tf_op jit(solution)/shard_map/ppermute | solution.py:582
  257.2 18.0 %collective-permute-start.49 = (bf16[216,768]{1,0:T(8,128)(2,1)S(1)}, bf16[216,768]{1,0:T(8,128)(2,1)S(1)}, u32[]{:S(2)}, u32[]{:S(2)}) collective-permute-start(bf16[216,768]{1,0:T(8,128)(2,1)S(1)} %copy-done.23), channel_id=1, source_target_pairs={{0,3},{1,0},{2,1},{3,2},{4,7},{5,4},{6,5},{7,6},{8,11},{9,8},{10,9... | collective-permute-start | bytes 995336 | tf_op jit(solution)/shard_map/ppermute | solution.py:582
  (30 other events, 163.3 us)
